TPU v7x, 1024 devices: a whole 8x8x8 slice. The times are simulated.
1024 devices in a mesh: grp: 64 (over x, z), sp: 16 (over y, core).
Axes of the slice: x: 8, y: 8, z: 8, core: 2. Of those that a mesh axis runs over, the one named last changes fastest.
Arguments:
- stay_qkv: bfloat16 [64, 2048, 3, 2048], P('grp', 'sp'), may hold values from -6 to 6
- outbox_qkv: bfloat16 [64, 128, 3, 2048], P('grp', 'sp'), may hold values from -6 to 6
- stay_clip: int32 [64, 2048], P('grp'), may hold values from 0 to 7, never falling along the last dimension, each value on 1 to 1024 neighbouring positions
- out_len: int32 [128], replicated, may hold values from 1 to 64, 6144 in all
- out_place: int32 [128], replicated, may hold values from 0 to 127, each once
Outputs:
- attn_stay: bfloat16 [64, 2048, 2048], P('grp', 'sp')
- attn_inbox: bfloat16 [64, 128, 2048], P('grp', 'sp')
Inputs may be any that keep to these rules, and one draw needn't show every extreme that they name: Each value appears once: clip j of group g goes to group out_place[2 g + j] // 2, inbox half out_place[2 g + j] % 2. Clip j of group g fills outbox rows j * 64 to j * 64 + out_len[2 g + j] - 1; the other rows of the half are unused. `stay_clip`: never falls along a group's tokens.
All inputs are finite; a program needn't handle non-finite values.
Results may differ from a plain program's by a relative error of at most 0.0043.
Values may be sent and summed in bfloat16 or wider, within the bound.
No kernel may reach another device: no remote copies, remote signals or barrier semaphores. Data moves between devices by JAX's collectives and lax.ppermute only.
A program may use at most 32 MiB of HBM per device.

v0:
```python
import math

import jax
import jax.numpy as jnp
from jax import lax
from jax.sharding import PartitionSpec as P

HEADS = 16
HD = 128


def attend(queries, key_rows, values, allowed):
    factor = 1.0 / math.sqrt(HD)
    scores = (
        jnp.einsum("qhd,khd->hqk", queries, key_rows, preferred_element_type=jnp.float32) * factor
    )
    scores = jnp.where(allowed[None], scores, -1e30)
    row_peak = jnp.max(scores, axis=2, keepdims=True)
    weights = jnp.exp(scores - row_peak)
    totals = jnp.sum(weights, axis=2)
    rounded = weights.astype(jnp.bfloat16)
    blended = jnp.einsum("hqk,khd->qhd", rounded, values, preferred_element_type=jnp.float32)
    return blended / jnp.transpose(totals)[:, :, None]


def half_attention(token_rows, length):
    position = jnp.arange(token_rows.shape[0], dtype=jnp.int32)
    usable = position < length
    allowed = usable[:, None] & usable[None, :]
    blended = attend(token_rows[:, 0], token_rows[:, 1], token_rows[:, 2], allowed)
    return jnp.where(usable[:, None, None], blended, jnp.zeros_like(blended)).astype(jnp.bfloat16)


def route_rows(piece, out_place, clip_slots, own_group, box_total):
    piece_rows = piece.shape[0]
    half_rows = box_total // 2
    token_index = jnp.arange(piece_rows, dtype=jnp.int32)
    source = token_index // box_total
    within = token_index % box_total
    clip_index = source * 2 + within // half_rows
    placed = jnp.sum(
        jnp.where(clip_index[:, None] == clip_slots[None, :], out_place[None, :], 0), axis=1
    )
    target = jnp.where(placed // 2 == own_group, placed % 2 * half_rows + within % half_rows, -1)
    selector = (jnp.arange(box_total, dtype=jnp.int32)[:, None] == target[None, :]).astype(
        jnp.bfloat16
    )
    return jnp.dot(selector, piece, preferred_element_type=jnp.float32)


def local(stay_qkv, outbox_qkv, stay_clip, out_len, out_place):
    stay_count = stay_qkv.shape[1]
    box_count = outbox_qkv.shape[1]
    feature_width = stay_qkv.shape[3]
    stay_local = stay_qkv[0].reshape(stay_count, 3, HEADS, HD)
    box_local = outbox_qkv[0].reshape(box_count, 3, HEADS, HD)
    stay_heads, box_heads = (
        lax.all_to_all(stay_local, "sp", split_axis=2, concat_axis=0, tiled=True),
        lax.all_to_all(box_local, "sp", split_axis=2, concat_axis=0, tiled=True),
    )
    group_rows = stay_heads.shape[0]
    box_total = box_heads.shape[0]
    half_rows = box_total // 2
    local_heads = stay_heads.shape[2]
    own_group = lax.axis_index("grp")
    clip_ids = stay_clip[0]
    block_rows = math.gcd(group_rows, 512)

    def stay_block(start):
        queries = lax.dynamic_slice_in_dim(stay_heads[:, 0], start, block_rows, 0)
        segment = lax.dynamic_slice_in_dim(clip_ids, start, block_rows, 0)
        allowed = segment[:, None] == clip_ids[None, :]
        return attend(queries, stay_heads[:, 1], stay_heads[:, 2], allowed).astype(jnp.bfloat16)

    starts = jnp.arange(group_rows // block_rows, dtype=jnp.int32) * block_rows
    stay_out = lax.map(stay_block, starts).reshape(group_rows, local_heads, HD)
    clip_slots = jnp.arange(out_place.shape[0], dtype=jnp.int32)
    flat_box = box_heads.reshape(box_total, 3 * local_heads * HD)
    moved = route_rows(
        lax.all_gather(flat_box, "grp", axis=0, tiled=True),
        out_place,
        clip_slots,
        own_group,
        box_total,
    )
    inbox = moved.astype(jnp.bfloat16).reshape(box_total, 3, local_heads, HD)
    pieces = []
    for half_index in range(2):
        length = jnp.sum(jnp.where(out_place == 2 * own_group + half_index, out_len, 0))
        pieces.append(
            half_attention(inbox[half_index * half_rows : (half_index + 1) * half_rows], length)
        )
    inbox_out = jnp.concatenate(pieces, axis=0)
    stay_back, inbox_back = (
        lax.all_to_all(stay_out, "sp", split_axis=0, concat_axis=1, tiled=True),
        lax.all_to_all(inbox_out, "sp", split_axis=0, concat_axis=1, tiled=True),
    )
    return (
        stay_back.reshape(1, stay_count, feature_width),
        inbox_back.reshape(1, box_count, feature_width),
    )


def solution(mesh):
    in_specs = (P("grp", "sp", None, None), P("grp", "sp", None, None), P("grp", None), P(), P())
    out_specs = (P("grp", "sp", None), P("grp", "sp", None))
    return jax.shard_map(local, mesh=mesh, in_specs=in_specs, out_specs=out_specs, check_vma=False)
```

profile of v0, /device:TPU:1, one launch (start us, length us, event | category | flops | bytes accessed | tf_op | source)
XLA Modules:
  0.0 158.3 jit_solution(17335359680472222215)
XLA Ops:
  7.2 0.0 all-gather.2.cloned.1.call-start
  7.2 0.9 copy.84
  8.2 25.8 %all_to_all.63 = bf16[8,3,16,128]{3,0,1,2:T(8,128)(2,1)} all-to-all(bf16[8,3,16,128]{3,0,1,2:T(8,128)(2,1)S(1)} %copy.38), channel_id=1, replica_groups=mesh['grp'=64,'sp'=16] {'sp'}, dimensions={2} | all-to-all | bytes 196608 | tf_op jit(solution)/shard_map/all_to_all | solution.py:59
  33.9 0.0 all-gather.2.cloned.1.call-update
  33.9 0.0 copy-start.1
  34.0 0.0 copy-start.2
  34.0 2.1 %copy.32 = bf16[1,128,3,2048]{1,3,2,0:T(8,128)(2,1)S(1)} copy(bf16[1,128,3,2048]{3,1,2,0:T(8,128)(2,1)} %param.7) | data formatting | bytes 3145728 | tf_op args[0]
  36.0 0.0 copy-start
  36.0 1.3 copy.33
  37.4 3.6 %all-to-all-start = ((bf16[128,3,16,128]{0,3,1,2:T(8,128)(2,1)}), bf16[128,3,16,128]{0,3,1,2:T(8,128)(2,1)S(1)}, u32[]{:S(2)}, u32[]{:S(2)}) async-start(bf16[128,3,16,128]{0,3,1,2:T(8,128)(2,1)} %copy.33), calls=%async_computation | async-start | bytes 3145728 | tf_op jit(solution)/shard_map/all_to_all | solution.py:58
  41.0 0.0 copy-done.1
  41.0 0.0 copy-done.2
  41.0 0.7 fusion.80
  41.7 1.3 iota_compare_fusion.5
  43.1 2.5 %select_reduce_fusion = s32[8192]{0:T(1024)S(1)} fusion(s32[128]{0:T(128)S(1)} %copy-done.1, s32[8192]{0:T(1024)S(1)} %fusion.47), kind=kLoop, calls=%fused_computation.18 | loop fusion | flops 3137536 | bytes 66048 | tf_op jit(solution)/shard_map/reduce_sum | solution.py:41
  45.7 33.6 %all-to-all-done = bf16[128,3,16,128]{0,3,1,2:T(8,128)(2,1)S(1)} async-done(((bf16[128,3,16,128]{0,3,1,2:T(8,128)(2,1)}), bf16[128,3,16,128]{0,3,1,2:T(8,128)(2,1)S(1)}, u32[]{:S(2)}, u32[]{:S(2)}) %all-to-all-start) | async-done | bytes 1572896 | tf_op jit(solution)/shard_map/all_to_all | solution.py:58
  79.3 0.9 copy.34
  80.2 0.0 copy-done
  80.2 22.0 %while.10 = (s32[]{:T(128)}, bf16[4,512,1,128]{3,1,2,0:T(8,128)(2,1)}, s32[4]{0:T(128)S(1)}, s32[2048]{0:T(1024)S(1)}, s32[1,2048]{1,0:T(1,128)S(1)}, /*index=5*...) while((s32[]{:T(128)}, bf16[4,512,1,128]{3,1,2,0:T(8,128)(2,1)}, s32[4]{0:T(128)S(1)}, ...), condition=%wide.region_3.4_spmd, body=%wide.region_0.3_spmd.sunk | while | flops 545389568 | bytes 14967443 | solution.py:76
  80.2 0.6 dynamic_slice.20
  82.5 0.1 dynamic_slice.21
  82.6 0.9 fusion.96
  83.6 0.7 fusion.97
  84.3 1.5 fusion.98
  85.7 0.6 dynamic_slice.20
  88.0 0.1 dynamic_slice.21
  88.2 0.9 fusion.96
  89.1 0.7 fusion.97
  89.8 1.5 fusion.98
  91.2 0.6 dynamic_slice.20
  93.5 0.1 dynamic_slice.21
  93.7 0.9 fusion.96
  94.6 0.7 fusion.97
  95.3 1.4 fusion.98
  96.7 0.6 dynamic_slice.20
  99.0 0.1 dynamic_slice.21
  99.2 0.9 fusion.96
  100.1 0.7 fusion.97
  100.8 1.5 fusion.98
  102.2 0.5 broadcast.272
  102.8 2.1 %reduce.12 = bf16[2048,128]{1,0:T(8,128)(2,1)S(1)} reduce(bf16[2048,1,128]{2,0,1:T(8,128)(2,1)} %bitcast.137, bf16[]{:T(256)} %broadcast.272), dimensions={1}, to_apply=%copy.36.reduce_sub_computation | reduce | bytes 1048578 | tf_op jit(solution)/shard_map/reshape | solution.py:76
  104.8 0.9 reshape.245
  105.7 4.3 %all-to-all-start.1 = ((bf16[16,2,8192]{2,1,0:T(2,128)(2,1)}), bf16[16,2,8192]{2,1,0:T(2,128)(2,1)S(1)}, u32[]{:S(2)}, u32[]{:S(2)}) async-start(bf16[16,2,8192]{2,1,0:T(2,128)(2,1)} %reshape.245), calls=%async_computation.1 | async-start | bytes 1048576 | tf_op jit(solution)/shard_map/all_to_all | solution.py:95
  110.0 18.8 %all-gather.2.cloned.1.call-done = bf16[8192,384]{1,0:T(8,128)(2,1)} async-done(((bf16[128,384]{1,0:T(8,128)(2,1)}), bf16[8192,384]{1,0:T(8,128)(2,1)}) %all-gather.2.cloned.1.call-update) | async-done | bytes 6291472 | tf_op jit(solution)/shard_map/all_gather | solution.py:80
  128.8 4.0 %fusion.29 = bf16[128,384]{1,0:T(8,128)(2,1)S(1)} fusion(bf16[8192,384]{1,0:T(8,128)(2,1)} %all-gather.2.cloned.1.call-done, s32[8192]{0:T(1024)S(1)} %fusion.51), kind=kOutput, calls=%fused_computation.23 | convolution fusion | flops 806404096 | bytes 6422528 | tf_op jit(solution)/shard_map/dot_general | solution.py:48
  132.8 0.1 fusion.84
  132.9 0.1 fusion.85
  133.0 0.2 fusion.87
  133.2 0.2 fusion.86
  133.4 0.2 fusion.35
  133.6 0.2 fusion.39
  133.9 0.7 reduce.13
  134.5 0.6 reshape.247
  135.2 0.0 all-to-all-done.1
  135.2 8.2 %all-to-all-start.3 = ((bf16[16,2,512]{2,1,0:T(2,128)(2,1)}), bf16[16,2,512]{2,1,0:T(2,128)(2,1)S(1)}, u32[]{:S(2)}, u32[]{:S(2)}) async-start(bf16[16,2,512]{2,1,0:T(2,128)(2,1)} %reshape.247), calls=%async_computation.3 | async-start | bytes 65536 | tf_op jit(solution)/shard_map/all_to_all | solution.py:96
  143.4 0.5 reshape.246
  143.9 0.1 copy.41
  144.0 0.3 copy.37
  144.3 1.0 copy.40
  145.3 5.5 %all-to-all-done.3 = bf16[16,2,512]{2,1,0:T(2,128)(2,1)S(1)} async-done(((bf16[16,2,512]{2,1,0:T(2,128)(2,1)}), bf16[16,2,512]{2,1,0:T(2,128)(2,1)S(1)}, u32[]{:S(2)}, u32[]{:S(2)}) %all-to-all-start.3) | async-done | bytes 32800 | tf_op jit(solution)/shard_map/all_to_all | solution.py:96
  150.8 0.6 copy.85
  (16 shorter events, 0.4 us)
Async XLA Ops:
  7.2 121.6 %all-gather.2.cloned.1.call-start = ((), (), s32[]{:S(2)}) async-start(), calls=%async_computation.4 | async-start | bytes 6389760 | tf_op jit(solution)/shard_map/all_gather | solution.py:80
  33.9 7.1 %copy-start.1 = (s32[128]{0:T(128)S(1)}, s32[128]{0:T(128)}, u32[]{:S(2)}) copy-start(s32[128]{0:T(128)} %param.11) | copy-start | bytes 1540
  34.0 7.1 %copy-start.2 = (s32[128]{0:T(128)S(1)}, s32[128]{0:T(128)}, u32[]{:S(2)}) copy-start(s32[128]{0:T(128)} %param.10) | copy-start | bytes 1540
  36.0 44.2 %copy-start = (s32[1,2048]{1,0:T(1,128)S(1)}, s32[1,2048]{1,0:T(1,128)}, u32[]{:S(2)}) copy-start(s32[1,2048]{1,0:T(1,128)} %param.9) | copy-start | bytes 24580
  37.4 41.9 %all-to-all-start = ((bf16[128,3,16,128]{0,3,1,2:T(8,128)(2,1)}), bf16[128,3,16,128]{0,3,1,2:T(8,128)(2,1)S(1)}, u32[]{:S(2)}, u32[]{:S(2)}) async-start(bf16[128,3,16,128]{0,3,1,2:T(8,128)(2,1)} %copy.33), calls=%async_computation | async-start | bytes 3145728 | tf_op jit(solution)/shard_map/all_to_all | solution.py:58
  105.7 29.4 %all-to-all-start.1 = ((bf16[16,2,8192]{2,1,0:T(2,128)(2,1)}), bf16[16,2,8192]{2,1,0:T(2,128)(2,1)S(1)}, u32[]{:S(2)}, u32[]{:S(2)}) async-start(bf16[16,2,8192]{2,1,0:T(2,128)(2,1)} %reshape.245), calls=%async_computation.1 | async-start | bytes 1048576 | tf_op jit(solution)/shard_map/all_to_all | solution.py:95
  135.2 15.6 %all-to-all-start.3 = ((bf16[16,2,512]{2,1,0:T(2,128)(2,1)}), bf16[16,2,512]{2,1,0:T(2,128)(2,1)S(1)}, u32[]{:S(2)}, u32[]{:S(2)}) async-start(bf16[16,2,512]{2,1,0:T(2,128)(2,1)} %reshape.247), calls=%async_computation.3 | async-start | bytes 65536 | tf_op jit(solution)/shard_map/all_to_all | solution.py:96
Sparse Core Ops, SparseCore 0:
  34.1 94.6 all-gather.1
where the time goes:
time: 159 us; the launch traced here: 158 us
  waiting for transfers between devices  57.9 us (36%)
  blocking collectives  25.8 us (16%)
  starting transfers between devices  16.1 us (10%)
  between operations  14.3 us (9%)
  matrix products  14.2 us (9%)
  local copies, waits for them, and re-layouts  12.8 us (8%)
  other arithmetic  10.3 us (6%)
  loops' own time  6.94 us (4%)
    all_to_all x1, waiting for transfers between devices, local(): lax.all_to_all(stay_local, 'sp', split_axis=2, concat_axis=0, tiled=True)  33.6 us
    all_to_all x1, blocking collectives, local(): lax.all_to_all(box_local, 'sp', split_axis=2, concat_axis=0, tiled=True)  25.8 us
    all_gather x1, waiting for transfers between devices, local(): lax.all_gather(flat_box, 'grp', axis=0, tiled=True)  18.8 us
    all_to_all x1, starting transfers between devices, local(): lax.all_to_all(inbox_out, 'sp', split_axis=0, concat_axis=1, tiled=True)  8.23 us
    another operation x1, loops' own time, local(): stay_out = lax.map(stay_block, starts).reshape(group_rows, local_heads, HD)  6.94 us
    unnamed x15, local copies, waits for them, and re-layouts  6.78 us
    dot_general x6, matrix products, attend(): jnp.einsum('hqk,khd->qhd', rounded, values, preferred_element_type=jnp.fl...  6.23 us
    all_to_all x1, waiting for transfers between devices, local(): lax.all_to_all(inbox_out, 'sp', split_axis=0, concat_axis=1, tiled=True)  5.49 us
  transfers between devices with their start and end apart: 4, of which 3 were waited for; matrix products, arithmetic and copies ran while one was open for 23% of the time, Pallas kernels for 0%

commit v1 on v0

v1 whole, which is shorter than its diff:
```python
import math

import jax
import jax.numpy as jnp
from jax import lax
from jax.experimental import pallas as pl
from jax.experimental.pallas import tpu as pltpu
from jax.sharding import Mesh
from jax.sharding import PartitionSpec as P

HEADS = 16
HD = 128
HALF = 64
ROWS = 256
BLOCKS = 8
WIDTHS = (2, 4, 5, 6, 8)
SCALE = math.log2(math.e) / math.sqrt(HD)
GRP = ("x", "z")
SP = ("y", "c")


def stay_kernel(low_ref, pick_ref, rows_ref, key_clip_ref, query_clip_ref, out_ref):
    def block(index, carry):
        queries = rows_ref[pl.ds(2 * index, 2), 0].reshape(ROWS, HD)
        query_clip = query_clip_ref[pl.ds(pl.multiple_of(index * ROWS, ROWS), ROWS), :]
        low = low_ref[index]

        def width(count):
            def run():
                scores, peak = [], None
                for j in range(count):
                    keys = rows_ref[pl.ds(2 * (low + j), 2), 1].reshape(ROWS, HD)
                    product = lax.dot_general(
                        queries, keys, (((1,), (1,)), ((), ())), preferred_element_type=jnp.float32
                    )
                    key_clip = key_clip_ref[low + j]
                    for part in (slice(0, HD), slice(HD, 2 * HD)):
                        score = jnp.where(query_clip == key_clip[:, part], product[:, part], -1e30)
                        peak = score if peak is None else jnp.maximum(peak, score)
                        scores.append(score)
                peak = jnp.broadcast_to(jnp.max(peak, axis=1, keepdims=True), (ROWS, HD))
                totals, blended = 0.0, 0.0
                for j in range(count):
                    left = jnp.exp2((scores[2 * j] - peak) * SCALE)
                    right = jnp.exp2((scores[2 * j + 1] - peak) * SCALE)
                    totals = totals + (left + right)
                    rounded = jnp.concatenate([left, right], axis=1).astype(jnp.bfloat16)
                    values = rows_ref[pl.ds(2 * (low + j), 2), 2].reshape(ROWS, HD)
                    blended = blended + jnp.dot(
                        rounded, values, preferred_element_type=jnp.float32
                    )
                result = blended / jnp.sum(totals, axis=1, keepdims=True)
                out_ref[pl.ds(2 * index, 2), 0:HD, :] = result.astype(jnp.bfloat16).reshape(
                    2, HD, HD
                )

            return run

        for number, count in enumerate(WIDTHS):
            pl.when(pick_ref[index] == number)(width(count))
        return carry

    lax.fori_loop(0, BLOCKS, block, 0)


def stay_plan(clip):
    blocks = clip.reshape(BLOCKS, ROWS)
    first, last = blocks[:, :1], blocks[:, -1:]
    low = jnp.sum((clip[None, :] < first).astype(jnp.int32), axis=1) // ROWS
    high = (jnp.sum((clip[None, :] <= last).astype(jnp.int32), axis=1) + ROWS - 1) // ROWS
    need = high - low
    pick = sum((need > count).astype(jnp.int32) for count in WIDTHS)
    count = sum(jnp.where(pick == number, value, 0) for number, value in enumerate(WIDTHS))
    key_clip = clip.reshape(BLOCKS, 1, ROWS)
    query_clip = jnp.broadcast_to(clip[:, None], (clip.shape[0], HD))
    return jnp.minimum(low, BLOCKS - count), pick, key_clip, query_clip


def stay_attention(plan, rows):
    smem, vmem = pl.BlockSpec(memory_space=pltpu.SMEM), pl.BlockSpec(memory_space=pltpu.VMEM)
    return pl.pallas_call(
        stay_kernel,
        out_shape=jax.ShapeDtypeStruct((HEADS, HD + 8, HD), jnp.bfloat16),
        in_specs=[smem, smem, vmem, vmem, vmem],
        out_specs=vmem,
        compiler_params=pltpu.CompilerParams(vmem_limit_bytes=40 * 2**20),
        name="stay_attention",
    )(plan[0], plan[1], rows, plan[2], plan[3])


def box_attention(rows, lengths):
    row = jnp.arange(2 * HALF, dtype=jnp.int32)
    usable = row % HALF < jnp.where(row < HALF, lengths[0], lengths[1])
    half = row // HALF
    allowed = (half[:, None] == half[None, :]) & usable[:, None] & usable[None, :]
    scores = lax.dot_general(
        rows[0], rows[1], (((1,), (1,)), ((), ())), preferred_element_type=jnp.float32
    )
    scores = jnp.where(allowed, scores, -1e30)
    weights = jnp.exp2((scores - jnp.max(scores, axis=1, keepdims=True)) * SCALE)
    totals = jnp.sum(weights, axis=1, keepdims=True)
    blended = jnp.dot(weights.astype(jnp.bfloat16), rows[2], preferred_element_type=jnp.float32)
    return jnp.where(usable[:, None], blended / totals, 0.0).astype(jnp.bfloat16)


def select_kernel(place_ref, here_ref, gathered_ref, slots_ref):
    x, z, c = here_ref[0], here_ref[1], here_ref[2]
    slots_ref[...] = jnp.zeros_like(slots_ref)
    for source in range(16):
        place = place_ref[2 * ((source // 2) * 8 + z) + source % 2]
        far = (place // 2) % 8 ^ z
        slot = (far % 2) * 8 + (far // 2 % 2) * 4 + (far // 4) * 2 + place % 2

        @pl.when(place // 16 == x)
        def _(source=source, slot=slot):
            clip = gathered_ref[2 * (source // 2) + c, source % 2]
            slots_ref[slot] = clip


def select(place, here, gathered):
    smem, vmem = pl.BlockSpec(memory_space=pltpu.SMEM), pl.BlockSpec(memory_space=pltpu.VMEM)
    return pl.pallas_call(
        select_kernel,
        out_shape=jax.ShapeDtypeStruct((16, HALF, HD), jnp.bfloat16),
        in_specs=[smem, smem, vmem],
        out_specs=vmem,
        name="select_clips",
    )(place, here, gathered)


def local(stay_qkv, outbox_qkv, stay_clip, out_len, out_place):
    x, z, c = lax.axis_index("x"), lax.axis_index("z"), lax.axis_index("c")
    group = x * 8 + z
    clip = stay_clip[0]

    box = jnp.transpose(outbox_qkv[0].reshape(8, 3, HEADS, HD), (2, 1, 0, 3))
    box = lax.all_to_all(box.reshape(HEADS, 24, HD), SP, split_axis=0, concat_axis=0, tiled=True)
    stay = jnp.transpose(stay_qkv[0].reshape(HD, 3, HEADS, HD), (2, 1, 0, 3))
    box, stay = lax.optimization_barrier((box, stay))
    stay = lax.all_to_all(
        stay.reshape(HEADS, 3 * HD, HD), SP, split_axis=0, concat_axis=0, tiled=True
    )

    box = jnp.transpose(box.reshape(HEADS, 3, 8, HD), (1, 0, 2, 3)).reshape(3, 2 * HALF, HD)
    lengths = lax.dynamic_slice_in_dim(out_len, 2 * group, 2)
    box_out = box_attention(box, lengths)

    gathered = lax.all_gather(box_out, ("x", "c"), axis=0, tiled=True)
    slots = select(out_place, jnp.stack([x, z, c]), gathered.reshape(16, 2, HALF, HD))
    for bit in (1, 2, 4):
        half = slots.shape[0] // 2
        came = lax.ppermute(slots[half:], "z", [(i, i ^ bit) for i in range(8)])
        slots = slots[:half] + came
    inbox = slots.reshape(HEADS, 8, HD)

    out = stay_attention(stay_plan(clip), stay.reshape(HEADS, 3, HD, HD))
    out = lax.dynamic_update_slice(out, inbox, (0, HD, 0))
    back = lax.all_to_all(out, SP, split_axis=0, concat_axis=0, tiled=True)
    stay_back = jnp.transpose(back[:, :HD], (1, 0, 2)).reshape(1, HD, HEADS * HD)
    inbox_back = jnp.transpose(back[:, HD:], (1, 0, 2)).reshape(1, 8, HEADS * HD)
    return stay_back, inbox_back


def solution(mesh):
    lines = Mesh(mesh.devices.reshape(8, 8, 8, 2), ("x", "z", "y", "c"))
    in_specs = (P(GRP, SP, None, None), P(GRP, SP, None, None), P(GRP, None), P(), P())
    out_specs = (P(GRP, SP, None), P(GRP, SP, None))
    return jax.shard_map(local, mesh=lines, in_specs=in_specs, out_specs=out_specs, check_vma=False)
```

time: 159 us -> 123 us (0.77)
  waiting for transfers between devices: 57.9 us -> 16.8 us
  starting transfers between devices: 16.1 us -> 35.4 us
  blocking collectives: 25.8 us -> 45 us
  matrix products: 14.2 us -> 0.39 us
  between operations: 14.3 us -> 0.79 us
  Pallas kernels: 0 us -> 9.34 us
  loops' own time: 6.94 us -> 0 us
  other arithmetic: 10.3 us -> 3.79 us
  local copies, waits for them, and re-layouts: 12.8 us -> 10.6 us
    all_to_all x3 -> x2, waiting for transfers between devices: 39.1 us -> 6.7 us  [the longest x1 6.69 us: local(): lax.all_to_all(box.reshape(HEADS, 24, HD), SP, split_axis=0, concat_axis=...]
    all_gather x1 -> x0, waiting for transfers between devices: 18.8 us -> none  [local(): lax.all_gather(flat_box, 'grp', axis=0, tiled=True)]
    all_gather x0 -> x1, blocking collectives: none -> 15.9 us  [local(): gathered = lax.all_gather(box_out, ('x', 'c'), axis=0, tiled=True)]
    ppermute x0 -> x3, starting transfers between devices: none -> 14.2 us  [local(): came = lax.ppermute(slots[half:], 'z', [(i, i ^ bit) for i in range(8)])]
    dot_general x13 -> x2, matrix products: 14.2 us -> 0.39 us  [the longest x1 0.22 us: box_attention(): jnp.dot(weights.astype(jnp.bfloat16), rows[2], preferred_element_type=jnp...]
    ppermute x0 -> x3, waiting for transfers between devices: none -> 10.1 us  [local(): came = lax.ppermute(slots[half:], 'z', [(i, i ^ bit) for i in range(8)])]
    pallas_call x0 -> x2, Pallas kernels: none -> 9.34 us  [the longest x1 7.09 us: stay_attention(): pl.pallas_call(stay_kernel, out_shape=jax.ShapeDtypeStruct((HEADS, HD + 8...]
    another operation x1 -> x0, loops' own time: 6.94 us -> none  [local(): stay_out = lax.map(stay_block, starts).reshape(group_rows, local_heads, HD)]
  transfers between devices with their start and end apart: 4 -> 5, of which waited for: 3 -> 4; matrix products, arithmetic and copies ran while one was open for 23% -> 8% of each run, Pallas kernels for 0% -> 2%
where the time goes in v1:
time: 123 us; the launch traced here: 122 us
  blocking collectives  45 us (37%)
  starting transfers between devices  35.4 us (29%)
  waiting for transfers between devices  16.8 us (14%)
  local copies, waits for them, and re-layouts  10.6 us (9%)
  Pallas kernels  9.34 us (8%)
  other arithmetic  3.79 us (3%)
    all_to_all x1, blocking collectives, local(): back = lax.all_to_all(out, SP, split_axis=0, concat_axis=0, tiled=True)  29.1 us
    all_to_all x1, starting transfers between devices, local(): lax.all_to_all(box.reshape(HEADS, 24, HD), SP, split_axis=0, concat_axis=...  17.4 us
    all_gather x1, blocking collectives, local(): gathered = lax.all_gather(box_out, ('x', 'c'), axis=0, tiled=True)  15.9 us
    ppermute x3, starting transfers between devices, local(): came = lax.ppermute(slots[half:], 'z', [(i, i ^ bit) for i in range(8)])  14.2 us
    ppermute x3, waiting for transfers between devices, local(): came = lax.ppermute(slots[half:], 'z', [(i, i ^ bit) for i in range(8)])  10.1 us
    pallas_call x1, Pallas kernels, stay_attention(): pl.pallas_call(stay_kernel, out_shape=jax.ShapeDtypeStruct((HEADS, HD + 8...  7.09 us
    all_to_all x1, waiting for transfers between devices, local(): lax.all_to_all(box.reshape(HEADS, 24, HD), SP, split_axis=0, concat_axis=...  6.69 us
    unnamed x10, local copies, waits for them, and re-layouts  4.42 us
  transfers between devices with their start and end apart: 5, of which 4 were waited for; matrix products, arithmetic and copies ran while one was open for 8% of the time, Pallas kernels for 2%

profile of v1, /device:TPU:1, one launch (start us, length us, event | category | flops | bytes accessed | tf_op | source)
XLA Modules:
  0.0 122.1 jit_solution(18263124609755602952)
XLA Ops:
  0.6 0.9 copy.42
  1.5 0.7 copy.43
  2.2 17.4 %all-to-all-start = ((bf16[16,24,128]{2,1,0:T(8,128)(2,1)}), bf16[16,24,128]{2,1,0:T(8,128)(2,1)S(1)}, u32[]{:S(2)}, u32[]{:S(2)}) async-start(bf16[16,24,128]{2,1,0:T(8,128)(2,1)} %bitcast.59), calls=%async_computation | async-start | bytes 196608 | tf_op jit(solution)/shard_map/all_to_all | solution.py:137
  19.7 1.8 %copy.39 = bf16[48,8,16,128]{3,2,1,0:T(8,128)(2,1)S(1)} copy(bf16[48,8,16,128]{3,1,2,0:T(8,128)(2,1)} %bitcast.67) | data formatting | bytes 3145728
  21.5 6.7 %all-to-all-done = bf16[16,24,128]{2,1,0:T(8,128)(2,1)S(1)} async-done(((bf16[16,24,128]{2,1,0:T(8,128)(2,1)}), bf16[16,24,128]{2,1,0:T(8,128)(2,1)S(1)}, u32[]{:S(2)}, u32[]{:S(2)}) %all-to-all-start) | async-done | bytes 98336 | tf_op jit(solution)/shard_map/all_to_all | solution.py:137
  28.2 1.6 %copy.30 = bf16[16,3,128,128]{3,2,1,0:T(8,128)(2,1)} copy(bf16[16,3,128,128]{3,0,2,1:T(8,128)(2,1)S(1)} %bitcast.64) | data formatting | bytes 3145728 | tf_op jit(solution)/shard_map/optimization_barrier | solution.py:139
  29.7 0.0 copy-start
  29.7 0.0 copy-start.1
  29.7 3.7 %all-to-all-start.1 = ((bf16[16,384,128]{2,1,0:T(8,128)(2,1)}), bf16[16,384,128]{2,1,0:T(8,128)(2,1)S(1)}, u32[]{:S(2)}, u32[]{:S(2)}) async-start(bf16[16,384,128]{2,1,0:T(8,128)(2,1)} %bitcast.6), calls=%async_computation.1 | async-start | bytes 3145728 | tf_op jit(solution)/shard_map/all_to_all | solution.py:140
  33.5 0.5 broadcast.189
  34.0 0.0 copy-done
  34.0 0.7 reduce.3
  34.7 0.0 copy-done.1
  34.7 0.1 dynamic_slice.3
  34.8 0.6 fusion.21
  35.4 1.3 %fusion.7 = pred[128]{0:T(512)(128)(4,1)S(1)} fusion(s32[]{:T(128)} %bitcast.13, s32[]{:T(128)} %bitcast.12), kind=kLoop, calls=%fused_computation.44 | loop fusion | flops 1152 | bytes 136 | tf_op jit(solution)/shard_map/lt | solution.py:93
  36.7 0.6 pad_add_fusion.here_ref
  37.3 0.2 fusion.22
  37.5 0.2 fusion.1
  37.7 15.9 %all_gather.3 = bf16[2048,128]{0,1:T(8,128)(2,1)S(1)} all-gather(bf16[128,128]{0,1:T(8,128)(2,1)S(1)} %fusion.1), channel_id=1, replica_groups=mesh['x'=8,'z'=8,'y'=8,'c'=2] {'x','c'}, dimensions={0}, use_global_device_ids=true | all-gather | bytes 557056 | tf_op jit(solution)/shard_map/all_gather | solution.py:148
  53.6 1.0 copy.32
  54.6 2.3 %select_clips.1 = bf16[16,64,128]{2,1,0:T(8,128)(2,1)} custom-call(s32[128]{0:T(128)} %place_ref.1, s32[3]{0:T(128)} %pad_add_fusion.here_ref, bf16[16,2,64,128]{3,2,1,0:T(8,128)(2,1)} %bitcast.65), custom_call_target="tpu_custom_call" | custom-call | tf_op jit(solution)/shard_map/select_clips/pallas_call | solution.py:122
  56.9 0.9 slice.69
  57.8 1.9 %collective-permute-start = (bf16[8,64,128]{2,1,0:T(8,128)(2,1)S(1)}, bf16[8,64,128]{2,1,0:T(8,128)(2,1)S(1)}, u32[]{:S(2)}, u32[]{:S(2)}) collective-permute-start(bf16[8,64,128]{2,1,0:T(8,128)(2,1)S(1)} %slice.69), channel_id=1, source_target_pairs={{0,16},{16,0},{32,48},{48,32},{64,80},{80,64},{96,112},{112,96},{1... | collective-permute-start | bytes 393224 | tf_op jit(solution)/shard_map/ppermute | solution.py:152
  59.7 0.1 fusion.20
  59.8 0.1 copy.36
  59.9 0.1 copy.37
  60.0 4.7 %collective-permute-done = bf16[8,64,128]{2,1,0:T(8,128)(2,1)S(1)} collective-permute-done((bf16[8,64,128]{2,1,0:T(8,128)(2,1)S(1)}, bf16[8,64,128]{2,1,0:T(8,128)(2,1)S(1)}, u32[]{:S(2)}, u32[]{:S(2)}) %collective-permute-start) | collective-permute-done | bytes 131104 | tf_op jit(solution)/shard_map/ppermute | solution.py:152
  64.6 0.9 slice_add_fusion
  65.6 3.4 %collective-permute-start.1 = (bf16[4,64,128]{2,1,0:T(8,128)(2,1)S(1)}, bf16[4,64,128]{2,1,0:T(8,128)(2,1)S(1)}, u32[]{:S(2)}, u32[]{:S(2)}) collective-permute-start(bf16[4,64,128]{2,1,0:T(8,128)(2,1)S(1)} %slice.71), channel_id=1, source_target_pairs={{0,32},{16,48},{32,0},{48,16},{64,96},{80,112},{96,64},{112,80},{1... | collective-permute-start | bytes 196616 | tf_op jit(solution)/shard_map/ppermute | solution.py:152
  69.0 0.2 convert_reduce_fusion
  69.2 4.1 %collective-permute-done.1 = bf16[4,64,128]{2,1,0:T(8,128)(2,1)S(1)} collective-permute-done((bf16[4,64,128]{2,1,0:T(8,128)(2,1)S(1)}, bf16[4,64,128]{2,1,0:T(8,128)(2,1)S(1)}, u32[]{:S(2)}, u32[]{:S(2)}) %collective-permute-start.1) | collective-permute-done | bytes 65568 | tf_op jit(solution)/shard_map/ppermute | solution.py:152
  73.4 8.9 %collective-permute-start.2 = (bf16[2,64,128]{2,1,0:T(8,128)(2,1)S(1)}, bf16[2,64,128]{2,1,0:T(8,128)(2,1)S(1)}, u32[]{:S(2)}, u32[]{:S(2)}) collective-permute-start(bf16[2,64,128]{2,1,0:T(8,128)(2,1)S(1)} %slice.73), channel_id=1, source_target_pairs={{0,64},{16,80},{32,96},{48,112},{64,0},{80,16},{96,32},{112,48},{1... | collective-permute-start | bytes 98312 | tf_op jit(solution)/shard_map/ppermute | solution.py:152
  82.3 1.3 %collective-permute-done.2 = bf16[2,64,128]{2,1,0:T(8,128)(2,1)S(1)} collective-permute-done((bf16[2,64,128]{2,1,0:T(8,128)(2,1)S(1)}, bf16[2,64,128]{2,1,0:T(8,128)(2,1)S(1)}, u32[]{:S(2)}, u32[]{:S(2)}) %collective-permute-start.2) | collective-permute-done | bytes 32800 | tf_op jit(solution)/shard_map/ppermute | solution.py:152
  83.6 0.0 all-to-all-done.1
  83.6 0.3 broadcast_in_dim.48.query_clip_ref
  83.9 7.1 %stay_attention.1 = bf16[16,136,128]{2,1,0:T(8,128)(2,1)S(1)} custom-call(s32[8]{0:T(128)S(1)} %get-tuple-element.14.low_ref, s32[8]{0:T(128)S(1)} %get-tuple-element.15.pick_ref, bf16[16,3,128,128]{3,2,1,0:T(8,128)(2,1)S(1)} %bitcast.60, s32[8,1,256]{2,1,0:T(1,128)S(1)} %bitcast.63, s32[2048,128]{1,0:T(8,128)S(1)} %broadcast_in_dim.48.query_clip_ref), custom_call_target="tpu_custom_call" | custom-call | tf_op jit(solution)/shard_map/stay_attention/pallas_call | solution.py:81
  91.0 29.1 %all_to_all.15 = bf16[16,136,128]{2,1,0:T(8,128)(2,1)S(1)} all-to-all(bf16[16,136,128]{2,1,0:T(8,128)(2,1)S(1)} %constant_dynamic-update-slice_fusion), channel_id=1, replica_groups=mesh['x'=8,'z'=8,'y'=8,'c'=2] {'y','c'}, dimensions={0} | all-to-all | bytes 1114112 | tf_op jit(solution)/shard_map/all_to_all | solution.py:158
  120.2 0.3 copy.33
  120.5 1.0 copy.34
  121.5 0.6 slice_bitcast_fusion.1
  (10 shorter events, 0.2 us)
Async XLA Ops:
  2.2 26.0 %all-to-all-start = ((bf16[16,24,128]{2,1,0:T(8,128)(2,1)}), bf16[16,24,128]{2,1,0:T(8,128)(2,1)S(1)}, u32[]{:S(2)}, u32[]{:S(2)}) async-start(bf16[16,24,128]{2,1,0:T(8,128)(2,1)} %bitcast.59), calls=%async_computation | async-start | bytes 196608 | tf_op jit(solution)/shard_map/all_to_all | solution.py:137
  29.7 4.3 %copy-start = (s32[1,2048]{1,0:T(1,128)S(1)}, s32[1,2048]{1,0:T(1,128)}, u32[]{:S(2)}) copy-start(s32[1,2048]{1,0:T(1,128)} %param.7) | copy-start | bytes 24580
  29.7 5.0 %copy-start.1 = (s32[128]{0:T(128)S(1)}, s32[128]{0:T(128)}, u32[]{:S(2)}) copy-start(s32[128]{0:T(128)} %param.8) | copy-start | bytes 1540
  29.7 53.8 %all-to-all-start.1 = ((bf16[16,384,128]{2,1,0:T(8,128)(2,1)}), bf16[16,384,128]{2,1,0:T(8,128)(2,1)S(1)}, u32[]{:S(2)}, u32[]{:S(2)}) async-start(bf16[16,384,128]{2,1,0:T(8,128)(2,1)} %bitcast.6), calls=%async_computation.1 | async-start | bytes 3145728 | tf_op jit(solution)/shard_map/all_to_all | solution.py:140
  57.8 6.8 %collective-permute-start = (bf16[8,64,128]{2,1,0:T(8,128)(2,1)S(1)}, bf16[8,64,128]{2,1,0:T(8,128)(2,1)S(1)}, u32[]{:S(2)}, u32[]{:S(2)}) collective-permute-start(bf16[8,64,128]{2,1,0:T(8,128)(2,1)S(1)} %slice.69), channel_id=1, source_target_pairs={{0,16},{16,0},{32,48},{48,32},{64,80},{80,64},{96,112},{112,96},{1... | collective-permute-start | bytes 393224 | tf_op jit(solution)/shard_map/ppermute | solution.py:152
  65.6 7.7 %collective-permute-start.1 = (bf16[4,64,128]{2,1,0:T(8,128)(2,1)S(1)}, bf16[4,64,128]{2,1,0:T(8,128)(2,1)S(1)}, u32[]{:S(2)}, u32[]{:S(2)}) collective-permute-start(bf16[4,64,128]{2,1,0:T(8,128)(2,1)S(1)} %slice.71), channel_id=1, source_target_pairs={{0,32},{16,48},{32,0},{48,16},{64,96},{80,112},{96,64},{112,80},{1... | collective-permute-start | bytes 196616 | tf_op jit(solution)/shard_map/ppermute | solution.py:152
  73.4 10.2 %collective-permute-start.2 = (bf16[2,64,128]{2,1,0:T(8,128)(2,1)S(1)}, bf16[2,64,128]{2,1,0:T(8,128)(2,1)S(1)}, u32[]{:S(2)}, u32[]{:S(2)}) collective-permute-start(bf16[2,64,128]{2,1,0:T(8,128)(2,1)S(1)} %slice.73), channel_id=1, source_target_pairs={{0,64},{16,80},{32,96},{48,112},{64,0},{80,16},{96,32},{112,48},{1... | collective-permute-start | bytes 98312 | tf_op jit(solution)/shard_map/ppermute | solution.py:152

commit v2 on v1

--- a/solution.py
+++ b/solution.py
@@ -4,6 +4,7 @@
 import jax.numpy as jnp
 from jax import lax
 from jax.experimental import pallas as pl
+from jax.experimental.layout import Layout, with_layout_constraint
 from jax.experimental.pallas import tpu as pltpu
 from jax.sharding import Mesh
 from jax.sharding import PartitionSpec as P
@@ -88,73 +89,105 @@
     )(plan[0], plan[1], rows, plan[2], plan[3])
 
 
-def box_attention(rows, lengths):
+def split_kernel(rows_ref, heads_ref):
+    for head in range(HEADS):
+        heads_ref[head, 0] = rows_ref[0, :, head * HD : (head + 1) * HD]
+
+
+def split_heads(rows):
+    tokens = rows.shape[1]
+    return pl.pallas_call(
+        split_kernel,
+        grid=(3,),
+        out_shape=jax.ShapeDtypeStruct((HEADS, 3, tokens, HD), rows.dtype),
+        in_specs=[pl.BlockSpec((1, tokens, HEADS * HD), lambda t: (t, 0, 0))],
+        out_specs=pl.BlockSpec((HEADS, 1, tokens, HD), lambda t: (0, t, 0, 0)),
+        compiler_params=pltpu.CompilerParams(vmem_limit_bytes=8 * 2**20),
+        name="split_heads",
+    )(rows)
+
+
+def box_mask(out_len):
+    group = lax.axis_index("x") * 8 + lax.axis_index("z")
+    lengths = lax.dynamic_slice_in_dim(out_len, 2 * group, 2)
     row = jnp.arange(2 * HALF, dtype=jnp.int32)
     usable = row % HALF < jnp.where(row < HALF, lengths[0], lengths[1])
     half = row // HALF
     allowed = (half[:, None] == half[None, :]) & usable[:, None] & usable[None, :]
+    return jnp.broadcast_to(usable[:, None], allowed.shape).astype(jnp.float32), jnp.where(
+        allowed, 0.0, 1.0
+    )
+
+
+def box_attention(masks, rows):
+    usable, blocked = masks
+    queries, keys, values = (rows[:, t].reshape(2 * HALF, HD) for t in range(3))
     scores = lax.dot_general(
-        rows[0], rows[1], (((1,), (1,)), ((), ())), preferred_element_type=jnp.float32
+        queries, keys, (((1,), (1,)), ((), ())), preferred_element_type=jnp.float32
     )
-    scores = jnp.where(allowed, scores, -1e30)
+    scores = jnp.where(blocked > 0.0, -1e30, scores)
     weights = jnp.exp2((scores - jnp.max(scores, axis=1, keepdims=True)) * SCALE)
     totals = jnp.sum(weights, axis=1, keepdims=True)
-    blended = jnp.dot(weights.astype(jnp.bfloat16), rows[2], preferred_element_type=jnp.float32)
-    return jnp.where(usable[:, None], blended / totals, 0.0).astype(jnp.bfloat16)
-
-
-def select_kernel(place_ref, here_ref, gathered_ref, slots_ref):
-    x, z, c = here_ref[0], here_ref[1], here_ref[2]
-    slots_ref[...] = jnp.zeros_like(slots_ref)
+    blended = jnp.dot(weights.astype(jnp.bfloat16), values, preferred_element_type=jnp.float32)
+    result = jnp.where(usable > 0.0, blended / totals, 0.0).astype(jnp.bfloat16)
+    return with_layout_constraint(result, Layout(major_to_minor=(0, 1)))
+
+
+def select_kernel(place_ref, gathered_ref, keep_ref, send_ref):
+    x, z, c = lax.axis_index("x"), lax.axis_index("z"), lax.axis_index("c")
+    keep_ref[...] = jnp.zeros_like(keep_ref)
+    send_ref[...] = jnp.zeros_like(send_ref)
     for source in range(16):
         place = place_ref[2 * ((source // 2) * 8 + z) + source % 2]
         far = (place // 2) % 8 ^ z
-        slot = (far % 2) * 8 + (far // 2 % 2) * 4 + (far // 4) * 2 + place % 2
-
-        @pl.when(place // 16 == x)
-        def _(source=source, slot=slot):
-            clip = gathered_ref[2 * (source // 2) + c, source % 2]
-            slots_ref[slot] = clip
-
-
-def select(place, here, gathered):
+        slot = (far // 2 % 2) * 4 + (far // 4) * 2 + place % 2
+        mine = place // 16 == x
+        for odd, slots_ref in enumerate((keep_ref, send_ref)):
+
+            @pl.when(mine & (far % 2 == odd))
+            def _(source=source, slot=slot, slots_ref=slots_ref):
+                slots_ref[slot] = gathered_ref[2 * (source // 2) + c, source % 2]
+
+
+def select(place, gathered):
     smem, vmem = pl.BlockSpec(memory_space=pltpu.SMEM), pl.BlockSpec(memory_space=pltpu.VMEM)
     return pl.pallas_call(
         select_kernel,
-        out_shape=jax.ShapeDtypeStruct((16, HALF, HD), jnp.bfloat16),
-        in_specs=[smem, smem, vmem],
-        out_specs=vmem,
+        out_shape=[jax.ShapeDtypeStruct((8, HALF, HD), jnp.bfloat16)] * 2,
+        in_specs=[smem, vmem],
+        out_specs=[vmem] * 2,
+        compiler_params=pltpu.CompilerParams(vmem_limit_bytes=4 * 2**20),
         name="select_clips",
-    )(place, here, gathered)
+    )(place, gathered)
+
+
+def swap(rows, bit):
+    return lax.ppermute(rows, "z", [(i, i ^ bit) for i in range(8)])
 
 
 def local(stay_qkv, outbox_qkv, stay_clip, out_len, out_place):
-    x, z, c = lax.axis_index("x"), lax.axis_index("z"), lax.axis_index("c")
-    group = x * 8 + z
-    clip = stay_clip[0]
-
+    masks = box_mask(out_len)
     box = jnp.transpose(outbox_qkv[0].reshape(8, 3, HEADS, HD), (2, 1, 0, 3))
     box = lax.all_to_all(box.reshape(HEADS, 24, HD), SP, split_axis=0, concat_axis=0, tiled=True)
-    stay = jnp.transpose(stay_qkv[0].reshape(HD, 3, HEADS, HD), (2, 1, 0, 3))
-    box, stay = lax.optimization_barrier((box, stay))
+    stay = split_heads(jnp.transpose(stay_qkv[0], (1, 0, 2)))
+    box, stay, masks = lax.optimization_barrier((box, stay, masks))
     stay = lax.all_to_all(
         stay.reshape(HEADS, 3 * HD, HD), SP, split_axis=0, concat_axis=0, tiled=True
     )
 
-    box = jnp.transpose(box.reshape(HEADS, 3, 8, HD), (1, 0, 2, 3)).reshape(3, 2 * HALF, HD)
-    lengths = lax.dynamic_slice_in_dim(out_len, 2 * group, 2)
-    box_out = box_attention(box, lengths)
+    box_out = box_attention(masks, box.reshape(HEADS, 3, 8, HD))
 
     gathered = lax.all_gather(box_out, ("x", "c"), axis=0, tiled=True)
-    slots = select(out_place, jnp.stack([x, z, c]), gathered.reshape(16, 2, HALF, HD))
-    for bit in (1, 2, 4):
-        half = slots.shape[0] // 2
-        came = lax.ppermute(slots[half:], "z", [(i, i ^ bit) for i in range(8)])
-        slots = slots[:half] + came
-    inbox = slots.reshape(HEADS, 8, HD)
-
-    out = stay_attention(stay_plan(clip), stay.reshape(HEADS, 3, HD, HD))
-    out = lax.dynamic_update_slice(out, inbox, (0, HD, 0))
+    keep, send = select(out_place, gathered.reshape(16, 2, HALF, HD))
+    slots = keep + swap(send, 1)
+    slots, clip = lax.optimization_barrier((slots, stay_clip[0]))
+    plan = stay_plan(clip)
+    slots = slots[:4] + swap(slots[4:], 2)
+    slots, stay, plan = lax.optimization_barrier((slots, stay, plan))
+    slots = slots[:2] + swap(slots[2:], 4)
+    out = stay_attention(plan, stay.reshape(HEADS, 3, HD, HD))
+
+    out = lax.dynamic_update_slice(out, slots.reshape(HEADS, 8, HD), (0, HD, 0))
     back = lax.all_to_all(out, SP, split_axis=0, concat_axis=0, tiled=True)
     stay_back = jnp.transpose(back[:, :HD], (1, 0, 2)).reshape(1, HD, HEADS * HD)
     inbox_back = jnp.transpose(back[:, HD:], (1, 0, 2)).reshape(1, 8, HEADS * HD)

time: 123 us -> 112 us (0.911)
  local copies, waits for them, and re-layouts: 10.6 us -> 6.28 us
  blocking collectives: 45 us -> 41.6 us
  starting transfers between devices: 35.4 us -> 33 us
  other arithmetic: 3.79 us -> 1.9 us
    all_to_all x1, waiting for transfers between devices: 0.01 us -> 6.09 us  [local(): lax.all_to_all(stay.reshape(HEADS, 3 * HD, HD), SP, split_axis=0, concat_...]
    all_to_all x1, waiting for transfers between devices: 6.69 us -> 3.09 us  [local(): lax.all_to_all(box.reshape(HEADS, 24, HD), SP, split_axis=0, concat_axis=...]
    all_to_all x1, blocking collectives: 29.1 us -> 25.7 us  [local(): back = lax.all_to_all(out, SP, split_axis=0, concat_axis=0, tiled=True)]
    ppermute x3, starting transfers between devices: 14.2 us -> 11.2 us  [swap(): return lax.ppermute(rows, 'z', [(i, i ^ bit) for i in range(8)])]
    optimization_barrier x1 -> x0, local copies, waits for them, and re-layouts: 1.56 us -> none  [local(): box, stay = lax.optimization_barrier((box, stay))]
    ppermute x3, waiting for transfers between devices: 10.1 us -> 8.68 us  [swap(): return lax.ppermute(rows, 'z', [(i, i ^ bit) for i in range(8)])]
    convert_element_type x0 -> x1, other arithmetic: none -> 1.29 us  [box_mask(): jnp.broadcast_to(usable[:, None], allowed.shape).astype(jnp.float32)]
    lt x1 -> x0, other arithmetic: 1.29 us -> none  [box_attention(): usable = row % HALF < jnp.where(row < HALF, lengths[0], lengths[1])]
  transfers between devices with their start and end apart: 5 -> 5, of which waited for: 4 -> 4; matrix products, arithmetic and copies ran while one was open for 8% -> 3% of each run, Pallas kernels for 2% -> 9%
where the time goes in v2:
time: 112 us
  blocking collectives  41.6 us (37%)
  starting transfers between devices  33 us (29%)
  waiting for transfers between devices  17.9 us (16%)
  Pallas kernels  9.88 us (9%)
  local copies, waits for them, and re-layouts  6.28 us (6%)
  other arithmetic  1.9 us (2%)
    all_to_all x1, blocking collectives, local(): back = lax.all_to_all(out, SP, split_axis=0, concat_axis=0, tiled=True)  25.7 us
    all_to_all x1, starting transfers between devices, local(): lax.all_to_all(box.reshape(HEADS, 24, HD), SP, split_axis=0, concat_axis=...  17.4 us
    all_gather x1, blocking collectives, local(): gathered = lax.all_gather(box_out, ('x', 'c'), axis=0, tiled=True)  15.9 us
    ppermute x3, starting transfers between devices, swap(): return lax.ppermute(rows, 'z', [(i, i ^ bit) for i in range(8)])  11.2 us
    ppermute x3, waiting for transfers between devices, swap(): return lax.ppermute(rows, 'z', [(i, i ^ bit) for i in range(8)])  8.68 us
    pallas_call x1, Pallas kernels, stay_attention(): pl.pallas_call(stay_kernel, out_shape=jax.ShapeDtypeStruct((HEADS, HD + 8...  6.86 us
    all_to_all x1, waiting for transfers between devices, local(): lax.all_to_all(stay.reshape(HEADS, 3 * HD, HD), SP, split_axis=0, concat_...  6.09 us
    all_to_all x1, starting transfers between devices, local(): lax.all_to_all(stay.reshape(HEADS, 3 * HD, HD), SP, split_axis=0, concat_...  4.33 us
  transfers between devices with their start and end apart: 5, of which 4 were waited for; matrix products, arithmetic and copies ran while one was open for 3% of the time, Pallas kernels for 9%

profile of v2, /device:TPU:1, one launch (start us, length us, event | category | flops | bytes accessed | tf_op | source)
XLA Modules:
  0.0 111.8 jit_solution(13996699056129452096)
XLA Ops:
  0.6 0.9 copy.23
  1.5 0.7 copy.24
  2.2 17.4 %all-to-all-start = ((bf16[16,24,128]{2,1,0:T(8,128)(2,1)}), bf16[16,24,128]{2,1,0:T(8,128)(2,1)S(1)}, u32[]{:S(2)}, u32[]{:S(2)}) async-start(bf16[16,24,128]{2,1,0:T(8,128)(2,1)} %bitcast.46), calls=%async_computation | async-start | bytes 196608 | tf_op jit(solution)/shard_map/all_to_all | solution.py:171
  19.7 0.0 copy-start
  19.7 1.4 %copy-done = bf16[1,128,3,2048]{3,1,2,0:T(8,128)(2,1)S(1)} copy-done((bf16[1,128,3,2048]{3,1,2,0:T(8,128)(2,1)S(1)}, bf16[1,128,3,2048]{3,1,2,0:T(8,128)(2,1)}, u32[]{:S(2)}) %copy-start) | copy-done | bytes 1572888
  21.1 0.0 copy-start.3
  21.1 1.9 %split_heads.1 = bf16[16,3,128,128]{3,2,1,0:T(8,128)(2,1)} custom-call(bf16[3,128,2048]{2,1,0:T(8,128)(2,1)S(1)} %bitcast.49), custom_call_target="tpu_custom_call" | custom-call | tf_op jit(solution)/shard_map/split_heads/pallas_call | solution.py:99
  23.0 0.0 copy-done.3
  23.0 0.1 dynamic_slice.3
  23.0 0.7 fusion.22
  23.7 1.3 %fusion.20 = (f32[128]{0:T(128)S(1)}, pred[128]{0:T(512)(128)(4,1)S(1)}) fusion(s32[]{:T(128)} %bitcast.5, s32[]{:T(128)} %bitcast.4), kind=kLoop, calls=%fused_computation.60 | loop fusion | flops 1280 | bytes 648 | tf_op jit(solution)/shard_map/convert_element_type | solution.py:117
  25.0 0.1 and_select_fusion
  25.1 3.1 %all-to-all-done = bf16[16,24,128]{2,1,0:T(8,128)(2,1)S(1)} async-done(((bf16[16,24,128]{2,1,0:T(8,128)(2,1)}), bf16[16,24,128]{2,1,0:T(8,128)(2,1)S(1)}, u32[]{:S(2)}, u32[]{:S(2)}) %all-to-all-start) | async-done | bytes 98336 | tf_op jit(solution)/shard_map/all_to_all | solution.py:171
  28.2 0.1 broadcast_in_dim.58
  28.2 0.0 copy-start.2
  28.3 4.3 %all-to-all-start.1 = ((bf16[16,384,128]{2,1,0:T(8,128)(2,1)}), bf16[16,384,128]{2,1,0:T(8,128)(2,1)S(1)}, u32[]{:S(2)}, u32[]{:S(2)}) async-start(bf16[16,384,128]{2,1,0:T(8,128)(2,1)} %bitcast.12), calls=%async_computation.1 | async-start | bytes 3145728 | tf_op jit(solution)/shard_map/all_to_all | solution.py:174
  32.6 0.0 copy-start.1
  32.6 0.2 fusion.23
  32.9 0.2 fusion.2
  33.0 0.2 fusion.1
  33.3 15.9 %all_gather.3 = bf16[2048,128]{1,0:T(8,128)(2,1)S(1)} all-gather(bf16[128,128]{1,0:T(8,128)(2,1)S(1)} %fusion.1), channel_id=1, replica_groups=mesh['x'=8,'z'=8,'y'=8,'c'=2] {'x','c'}, dimensions={0}, use_global_device_ids=true | all-gather | bytes 557056 | tf_op jit(solution)/shard_map/all_gather | solution.py:180
  49.2 0.0 copy-done.2
  49.2 1.1 %select_clips.1 = (bf16[8,64,128]{2,1,0:T(8,128)(2,1)S(1)}, bf16[8,64,128]{2,1,0:T(8,128)(2,1)S(1)}) custom-call(s32[128]{0:T(128)S(1)} %copy-done.2, bf16[16,2,64,128]{3,2,1,0:T(8,128)(2,1)S(1)} %bitcast.48), custom_call_target="tpu_custom_call" | custom-call | tf_op jit(solution)/shard_map/select_clips/pallas_call | solution.py:154
  50.3 1.9 %collective-permute-start = (bf16[8,64,128]{2,1,0:T(8,128)(2,1)S(1)}, bf16[8,64,128]{2,1,0:T(8,128)(2,1)S(1)}, u32[]{:S(2)}, u32[]{:S(2)}) collective-permute-start(bf16[8,64,128]{2,1,0:T(8,128)(2,1)S(1)} %get-tuple-element.20), channel_id=1, source_target_pairs={{0,16},{16,0},{32,48},{48,32},{64,80},{80,64},{96,112},{112,96},{1... | collective-permute-start | bytes 393224 | tf_op jit(solution)/shard_map/ppermute | solution.py:165
  52.3 4.9 %collective-permute-done = bf16[8,64,128]{2,1,0:T(8,128)(2,1)S(1)} collective-permute-done((bf16[8,64,128]{2,1,0:T(8,128)(2,1)S(1)}, bf16[8,64,128]{2,1,0:T(8,128)(2,1)S(1)}, u32[]{:S(2)}, u32[]{:S(2)}) %collective-permute-start) | collective-permute-done | bytes 131104 | tf_op jit(solution)/shard_map/ppermute | solution.py:165
  57.2 3.4 %collective-permute-start.1 = (bf16[4,64,128]{2,1,0:T(8,128)(2,1)S(1)}, bf16[4,64,128]{2,1,0:T(8,128)(2,1)S(1)}, u32[]{:S(2)}, u32[]{:S(2)}) collective-permute-start(bf16[4,64,128]{2,1,0:T(8,128)(2,1)S(1)} %slice.45), channel_id=1, source_target_pairs={{0,32},{16,48},{32,0},{48,16},{64,96},{80,112},{96,64},{112,80},{1... | collective-permute-start | bytes 196616 | tf_op jit(solution)/shard_map/ppermute | solution.py:165
  60.7 0.0 copy-done.1
  60.7 0.2 slice_reduce_fusion
  60.9 0.2 convert_reduce_fusion
  61.2 3.8 %collective-permute-done.1 = bf16[4,64,128]{2,1,0:T(8,128)(2,1)S(1)} collective-permute-done((bf16[4,64,128]{2,1,0:T(8,128)(2,1)S(1)}, bf16[4,64,128]{2,1,0:T(8,128)(2,1)S(1)}, u32[]{:S(2)}, u32[]{:S(2)}) %collective-permute-start.1) | collective-permute-done | bytes 65568 | tf_op jit(solution)/shard_map/ppermute | solution.py:165
  64.9 6.1 %all-to-all-done.1 = bf16[16,384,128]{2,1,0:T(8,128)(2,1)S(1)} async-done(((bf16[16,384,128]{2,1,0:T(8,128)(2,1)}), bf16[16,384,128]{2,1,0:T(8,128)(2,1)S(1)}, u32[]{:S(2)}, u32[]{:S(2)}) %all-to-all-start.1) | async-done | bytes 1572896 | tf_op jit(solution)/shard_map/all_to_all | solution.py:174
  71.0 0.3 broadcast_in_dim.63.query_clip_ref
  71.4 5.9 %collective-permute-start.2 = (bf16[2,64,128]{2,1,0:T(8,128)(2,1)S(1)}, bf16[2,64,128]{2,1,0:T(8,128)(2,1)S(1)}, u32[]{:S(2)}, u32[]{:S(2)}) collective-permute-start(bf16[2,64,128]{2,1,0:T(8,128)(2,1)S(1)} %slice.49), channel_id=1, source_target_pairs={{0,64},{16,80},{32,96},{48,112},{64,0},{80,16},{96,32},{112,48},{1... | collective-permute-start | bytes 98312 | tf_op jit(solution)/shard_map/ppermute | solution.py:165
  77.3 6.9 %stay_attention.1 = bf16[16,136,128]{2,1,0:T(8,128)(2,1)S(1)} custom-call(s32[8]{0:T(128)S(1)} %get-tuple-element.24.low_ref, s32[8]{0:T(128)S(1)} %get-tuple-element.25.pick_ref, bf16[16,3,128,128]{3,2,1,0:T(8,128)(2,1)S(1)} %bitcast.47, s32[8,1,256]{2,1,0:T(1,128)S(1)} %bitcast.53, s32[2048,128]{1,0:T(8,128)S(1)} %broadcast_in_dim.63.query_clip_ref), custom_call_target="tpu_custom_call" | custom-call | tf_op jit(solution)/shard_map/stay_attention/pallas_call | solution.py:82
  84.1 0.0 collective-permute-done.2
  84.2 25.7 %all_to_all.15 = bf16[16,136,128]{2,1,0:T(8,128)(2,1)S(1)} all-to-all(bf16[16,136,128]{2,1,0:T(8,128)(2,1)S(1)} %constant_dynamic-update-slice_fusion), channel_id=1, replica_groups=mesh['x'=8,'z'=8,'y'=8,'c'=2] {'y','c'}, dimensions={0} | all-to-all | bytes 1114112 | tf_op jit(solution)/shard_map/all_to_all | solution.py:191
  109.9 0.3 copy.17
  110.2 1.0 copy.18
  111.2 0.6 slice_bitcast_fusion.1
  (10 shorter events, 0.2 us)
Async XLA Ops:
  2.2 26.0 %all-to-all-start = ((bf16[16,24,128]{2,1,0:T(8,128)(2,1)}), bf16[16,24,128]{2,1,0:T(8,128)(2,1)S(1)}, u32[]{:S(2)}, u32[]{:S(2)}) async-start(bf16[16,24,128]{2,1,0:T(8,128)(2,1)} %bitcast.46), calls=%async_computation | async-start | bytes 196608 | tf_op jit(solution)/shard_map/all_to_all | solution.py:171
  19.7 1.4 %copy-start = (bf16[1,128,3,2048]{3,1,2,0:T(8,128)(2,1)S(1)}, bf16[1,128,3,2048]{3,1,2,0:T(8,128)(2,1)}, u32[]{:S(2)}) copy-start(bf16[1,128,3,2048]{3,1,2,0:T(8,128)(2,1)} %param.5) | copy-start | bytes 4718596
  21.1 1.9 %copy-start.3 = (s32[128]{0:T(128)S(1)}, s32[128]{0:T(128)}, u32[]{:S(2)}) copy-start(s32[128]{0:T(128)} %param.8) | copy-start | bytes 1540
  28.2 20.9 %copy-start.2 = (s32[128]{0:T(128)S(1)}, s32[128]{0:T(128)}, u32[]{:S(2)}) copy-start(s32[128]{0:T(128)} %place_ref.1) | copy-start | bytes 1540
  28.3 42.8 %all-to-all-start.1 = ((bf16[16,384,128]{2,1,0:T(8,128)(2,1)}), bf16[16,384,128]{2,1,0:T(8,128)(2,1)S(1)}, u32[]{:S(2)}, u32[]{:S(2)}) async-start(bf16[16,384,128]{2,1,0:T(8,128)(2,1)} %bitcast.12), calls=%async_computation.1 | async-start | bytes 3145728 | tf_op jit(solution)/shard_map/all_to_all | solution.py:174
  32.6 28.1 %copy-start.1 = (s32[1,2048]{1,0:T(1,128)S(1)}, s32[1,2048]{1,0:T(1,128)}, u32[]{:S(2)}) copy-start(s32[1,2048]{1,0:T(1,128)} %param.7) | copy-start | bytes 24580
  50.3 6.8 %collective-permute-start = (bf16[8,64,128]{2,1,0:T(8,128)(2,1)S(1)}, bf16[8,64,128]{2,1,0:T(8,128)(2,1)S(1)}, u32[]{:S(2)}, u32[]{:S(2)}) collective-permute-start(bf16[8,64,128]{2,1,0:T(8,128)(2,1)S(1)} %get-tuple-element.20), channel_id=1, source_target_pairs={{0,16},{16,0},{32,48},{48,32},{64,80},{80,64},{96,112},{112,96},{1... | collective-permute-start | bytes 393224 | tf_op jit(solution)/shard_map/ppermute | solution.py:165
  57.2 7.7 %collective-permute-start.1 = (bf16[4,64,128]{2,1,0:T(8,128)(2,1)S(1)}, bf16[4,64,128]{2,1,0:T(8,128)(2,1)S(1)}, u32[]{:S(2)}, u32[]{:S(2)}) collective-permute-start(bf16[4,64,128]{2,1,0:T(8,128)(2,1)S(1)} %slice.45), channel_id=1, source_target_pairs={{0,32},{16,48},{32,0},{48,16},{64,96},{80,112},{96,64},{112,80},{1... | collective-permute-start | bytes 196616 | tf_op jit(solution)/shard_map/ppermute | solution.py:165
  71.4 12.8 %collective-permute-start.2 = (bf16[2,64,128]{2,1,0:T(8,128)(2,1)S(1)}, bf16[2,64,128]{2,1,0:T(8,128)(2,1)S(1)}, u32[]{:S(2)}, u32[]{:S(2)}) collective-permute-start(bf16[2,64,128]{2,1,0:T(8,128)(2,1)S(1)} %slice.49), channel_id=1, source_target_pairs={{0,64},{16,80},{32,96},{48,112},{64,0},{80,16},{96,32},{112,48},{1... | collective-permute-start | bytes 98312 | tf_op jit(solution)/shard_map/ppermute | solution.py:165

commit v3 on v2

v3 whole, which is shorter than its diff:
```python
import math

import jax
import jax.numpy as jnp
from jax import lax
from jax.experimental import pallas as pl
from jax.experimental.layout import Layout, with_layout_constraint
from jax.experimental.pallas import tpu as pltpu
from jax.sharding import Mesh
from jax.sharding import PartitionSpec as P

HEADS = 16
HD = 128
HALF = 64
ROWS = 256
BLOCKS = 8
WIDTHS = (2, 3, 4, 5, 6, 8)
SCALE = math.log2(math.e) / math.sqrt(HD)
GRP = ("x", "z")
SP = ("y", "c")


def stay_kernel(low_ref, pick_ref, rows_ref, key_clip_ref, query_clip_ref, out_ref):
    def score(index, count):
        queries = rows_ref[pl.ds(2 * index, 2), 0].reshape(ROWS, HD)
        query_clip = query_clip_ref[pl.ds(pl.multiple_of(index * ROWS, ROWS), ROWS), :]
        low = low_ref[index]
        scores, peak = [], None
        for j in range(count):
            keys = rows_ref[pl.ds(2 * (low + j), 2), 1].reshape(ROWS, HD)
            product = lax.dot_general(
                queries, keys, (((1,), (1,)), ((), ())), preferred_element_type=jnp.float32
            )
            key_clip = key_clip_ref[low + j]
            for part in (slice(0, HD), slice(HD, 2 * HD)):
                masked = jnp.where(query_clip == key_clip[:, part], product[:, part], -1e30)
                peak = masked if peak is None else jnp.maximum(peak, masked)
                scores.append(masked)
        peak = jnp.broadcast_to(jnp.max(peak, axis=1, keepdims=True), (ROWS, HD))
        return low, scores, peak

    def blend(index, count, low, scores, peak):
        totals, blended = 0.0, 0.0
        for j in range(count):
            left = jnp.exp2((scores[2 * j] - peak) * SCALE)
            right = jnp.exp2((scores[2 * j + 1] - peak) * SCALE)
            totals = totals + (left + right)
            rounded = jnp.concatenate([left, right], axis=1).astype(jnp.bfloat16)
            values = rows_ref[pl.ds(2 * (low + j), 2), 2].reshape(ROWS, HD)
            blended = blended + jnp.dot(rounded, values, preferred_element_type=jnp.float32)
        result = blended / jnp.sum(totals, axis=1, keepdims=True)
        out_ref[pl.ds(2 * index, 2), 0:HD, :] = result.astype(jnp.bfloat16).reshape(2, HD, HD)

    def pair(number, carry):
        def width(count):
            def run():
                first = score(2 * number, count)
                second = score(2 * number + 1, count)
                blend(2 * number, count, *first)
                blend(2 * number + 1, count, *second)

            return run

        for choice, count in enumerate(WIDTHS):
            pl.when(pick_ref[number] == choice)(width(count))
        return carry

    lax.fori_loop(0, BLOCKS // 2, pair, 0)


def plan_kernel(edge_ref, clip_ref, low_ref, pick_ref, query_clip_ref):
    clip = clip_ref[...]

    def number(mask):
        return jnp.sum(jnp.where(mask, 1.0, 0.0)).astype(jnp.int32)

    for pair in range(BLOCKS // 2):
        lows, needs = [], []
        for index in (2 * pair, 2 * pair + 1):
            first, last = edge_ref[0, index * ROWS], edge_ref[0, (index + 1) * ROWS - 1]
            low = number(clip < first) >> 8
            lows.append(low)
            needs.append(((number(clip <= last) + ROWS - 1) >> 8) - low)
        need = jnp.maximum(needs[0], needs[1])
        pick, count = jnp.int32(0), jnp.int32(WIDTHS[0])
        for choice, width in enumerate(WIDTHS[:-1]):
            pick = jnp.where(need > width, choice + 1, pick)
            count = jnp.where(need > width, WIDTHS[choice + 1], count)
        pick_ref[pair] = pick
        for index, low in zip((2 * pair, 2 * pair + 1), lows):
            low_ref[index] = jnp.minimum(low, BLOCKS - count)
    for index in range(BLOCKS):
        row = jnp.broadcast_to(clip[index : index + 1], (HD, ROWS))
        query_clip_ref[index * ROWS : (index + 1) * ROWS, :] = jnp.transpose(row)


def stay_plan(clip):
    smem, vmem = pl.BlockSpec(memory_space=pltpu.SMEM), pl.BlockSpec(memory_space=pltpu.VMEM)
    blocks = clip.reshape(BLOCKS, ROWS)
    low, pick, query_clip = pl.pallas_call(
        plan_kernel,
        out_shape=[
            jax.ShapeDtypeStruct((BLOCKS,), jnp.int32),
            jax.ShapeDtypeStruct((BLOCKS // 2,), jnp.int32),
            jax.ShapeDtypeStruct((BLOCKS * ROWS, HD), jnp.int32),
        ],
        in_specs=[smem, vmem],
        out_specs=[smem, smem, vmem],
        compiler_params=pltpu.CompilerParams(vmem_limit_bytes=8 * 2**20),
        cost_estimate=pl.CostEstimate(flops=10**7, bytes_accessed=2**20, transcendentals=0),
        name="stay_plan",
    )(clip, blocks)
    return low, pick, blocks.reshape(BLOCKS, 1, ROWS), query_clip


def stay_attention(plan, rows):
    smem, vmem = pl.BlockSpec(memory_space=pltpu.SMEM), pl.BlockSpec(memory_space=pltpu.VMEM)
    return pl.pallas_call(
        stay_kernel,
        out_shape=jax.ShapeDtypeStruct((HEADS, HD + 8, HD), jnp.bfloat16),
        in_specs=[smem, smem, vmem, vmem, vmem],
        out_specs=vmem,
        compiler_params=pltpu.CompilerParams(vmem_limit_bytes=40 * 2**20),
        name="stay_attention",
    )(plan[0], plan[1], rows, plan[2], plan[3])


def split_kernel(length_ref, rows_ref, heads_ref, mask_ref):
    for head in range(HEADS):
        heads_ref[head, 0] = rows_ref[0, :, head * HD : (head + 1) * HD]

    @pl.when(pl.program_id(0) == 0)
    def _():
        group = lax.axis_index("x") * 8 + lax.axis_index("z")
        first, second = length_ref[2 * group], length_ref[2 * group + 1]

        def limits(axis):
            row = lax.broadcasted_iota(jnp.int32, (2 * HALF, 2 * HALF), axis)
            return row // HALF, row % HALF < jnp.where(row < HALF, first, second)

        query_half, query_usable = limits(0)
        key_half, key_usable = limits(1)
        allowed = (query_half == key_half) & query_usable & key_usable
        mask_ref[0] = jnp.where(query_usable, 1.0, 0.0)
        mask_ref[1] = jnp.where(allowed, 0.0, 1.0)


def split_heads(out_len, rows):
    return pl.pallas_call(
        split_kernel,
        grid=(3,),
        out_shape=[
            jax.ShapeDtypeStruct((HEADS, 3, HD, HD), rows.dtype),
            jax.ShapeDtypeStruct((2, 2 * HALF, 2 * HALF), jnp.float32),
        ],
        in_specs=[
            pl.BlockSpec(memory_space=pltpu.SMEM),
            pl.BlockSpec((1, HD, HEADS * HD), lambda t: (t, 0, 0)),
        ],
        out_specs=[
            pl.BlockSpec((HEADS, 1, HD, HD), lambda t: (0, t, 0, 0)),
            pl.BlockSpec((2, 2 * HALF, 2 * HALF), lambda t: (0, 0, 0)),
        ],
        compiler_params=pltpu.CompilerParams(vmem_limit_bytes=48 * 2**20),
        name="split_heads",
    )(out_len, rows)


def merge_kernel(back_ref, stay_ref, inbox_ref):
    for head in range(HEADS):
        columns = slice(head * HD, (head + 1) * HD)
        stay_ref[:, columns] = back_ref[head, 0:HD, :]
        inbox_ref[:, columns] = back_ref[head, HD : HD + 8, :]


def merge_heads(back):
    return pl.pallas_call(
        merge_kernel,
        out_shape=[
            jax.ShapeDtypeStruct((HD, HEADS * HD), back.dtype),
            jax.ShapeDtypeStruct((8, HEADS * HD), back.dtype),
        ],
        in_specs=[pl.BlockSpec(memory_space=pltpu.VMEM)],
        out_specs=[pl.BlockSpec(memory_space=pltpu.VMEM)] * 2,
        compiler_params=pltpu.CompilerParams(vmem_limit_bytes=8 * 2**20),
        name="merge_heads",
    )(back)


def box_attention(masks, rows):
    usable, blocked = masks
    queries, keys, values = (rows[:, t].reshape(2 * HALF, HD) for t in range(3))
    scores = lax.dot_general(
        queries, keys, (((1,), (1,)), ((), ())), preferred_element_type=jnp.float32
    )
    scores = jnp.where(blocked > 0.0, -1e30, scores)
    weights = jnp.exp2((scores - jnp.max(scores, axis=1, keepdims=True)) * SCALE)
    totals = jnp.sum(weights, axis=1, keepdims=True)
    blended = jnp.dot(weights.astype(jnp.bfloat16), values, preferred_element_type=jnp.float32)
    result = jnp.where(usable > 0.0, blended / totals, 0.0).astype(jnp.bfloat16)
    return with_layout_constraint(result, Layout(major_to_minor=(0, 1)))


def select_kernel(place_ref, gathered_ref, keep_ref, send_ref):
    x, z, c = lax.axis_index("x"), lax.axis_index("z"), lax.axis_index("c")
    keep_ref[...] = jnp.zeros_like(keep_ref)
    send_ref[...] = jnp.zeros_like(send_ref)
    for source in range(16):
        place = place_ref[2 * ((source // 2) * 8 + z) + source % 2]
        far = (place // 2) % 8 ^ z
        slot = (far // 2 % 2) * 4 + (far // 4) * 2 + place % 2
        mine = place // 16 == x
        for odd, slots_ref in enumerate((keep_ref, send_ref)):

            @pl.when(mine & (far % 2 == odd))
            def _(source=source, slot=slot, slots_ref=slots_ref):
                slots_ref[slot] = gathered_ref[2 * (source // 2) + c, source % 2]


def select(place, gathered):
    smem, vmem = pl.BlockSpec(memory_space=pltpu.SMEM), pl.BlockSpec(memory_space=pltpu.VMEM)
    return pl.pallas_call(
        select_kernel,
        out_shape=[jax.ShapeDtypeStruct((8, HALF, HD), jnp.bfloat16)] * 2,
        in_specs=[smem, vmem],
        out_specs=[vmem] * 2,
        compiler_params=pltpu.CompilerParams(vmem_limit_bytes=4 * 2**20),
        name="select_clips",
    )(place, gathered)


def swap(rows, bit):
    return lax.ppermute(rows, "z", [(i, i ^ bit) for i in range(8)])


def local(stay_qkv, outbox_qkv, stay_clip, out_len, out_place):
    box = jnp.transpose(outbox_qkv[0].reshape(8, 3, HEADS, HD), (2, 1, 0, 3))
    box = with_layout_constraint(box.reshape(HEADS, 24, HD), Layout(major_to_minor=(0, 1, 2)))
    box = lax.all_to_all(box, SP, split_axis=0, concat_axis=0, tiled=True)
    stay, masks = split_heads(out_len, jnp.transpose(stay_qkv[0], (1, 0, 2)))
    box, stay = lax.optimization_barrier((box, stay))
    stay = lax.all_to_all(
        stay.reshape(HEADS, 3 * HD, HD), SP, split_axis=0, concat_axis=0, tiled=True
    )

    box_out = box_attention(masks, box.reshape(HEADS, 3, 8, HD))

    gathered = lax.all_gather(box_out, ("x", "c"), axis=0, tiled=True)
    keep, send = select(out_place, gathered.reshape(16, 2, HALF, HD))
    send, clip = lax.optimization_barrier((send, stay_clip))
    came, plan = lax.optimization_barrier((swap(send, 1), stay_plan(clip)))
    slots = keep + came
    came = swap(slots[4:], 2)
    slots = slots[:4] + came
    came = swap(slots[2:], 4)

    out = stay_attention(plan, stay.reshape(HEADS, 3, HD, HD))
    out, slots = lax.optimization_barrier((out, slots))
    inbox = (slots[:2] + came).reshape(HEADS, 8, HD)
    out = lax.dynamic_update_slice(out, inbox, (0, HD, 0))
    stay_back, inbox_back = merge_heads(
        lax.all_to_all(out, SP, split_axis=0, concat_axis=0, tiled=True)
    )
    return stay_back[None], inbox_back[None]


def solution(mesh):
    lines = Mesh(mesh.devices.reshape(8, 8, 8, 2), ("x", "z", "y", "c"))
    in_specs = (P(GRP, SP, None, None), P(GRP, SP, None, None), P(GRP, None), P(), P())
    out_specs = (P(GRP, SP, None), P(GRP, SP, None))
    return jax.shard_map(local, mesh=lines, in_specs=in_specs, out_specs=out_specs, check_vma=False)
```

time: 112 us -> 109 us (0.973)
  waiting for transfers between devices: 17.9 us -> 10.7 us
  starting transfers between devices: 33 us -> 35.7 us
  blocking collectives: 41.6 us -> 44.1 us
  local copies, waits for them, and re-layouts: 6.28 us -> 4.16 us
  Pallas kernels: 9.88 us -> 11.6 us
    all_to_all x1, waiting for transfers between devices: 6.09 us -> 0.01 us  [local(): lax.all_to_all(stay.reshape(HEADS, 3 * HD, HD), SP, split_axis=0, concat_...]
    ppermute x3, starting transfers between devices: 11.2 us -> 14.5 us  [swap(): return lax.ppermute(rows, 'z', [(i, i ^ bit) for i in range(8)])]
    pallas_call x1 -> x3, Pallas kernels: 1.87 us -> 4.81 us  [the longest x1 2.41 us: split_heads(): pl.pallas_call(split_kernel, grid=(3,), out_shape=[jax.ShapeDtypeStruct((...]
    all_to_all x1, blocking collectives: 25.7 us -> 28.2 us  [local(): lax.all_to_all(out, SP, split_axis=0, concat_axis=0, tiled=True)]
    ppermute x3, waiting for transfers between devices: 8.68 us -> 6.61 us  [swap(): return lax.ppermute(rows, 'z', [(i, i ^ bit) for i in range(8)])]
    convert_element_type x1 -> x0, other arithmetic: 1.29 us -> none  [box_mask(): jnp.broadcast_to(usable[:, None], allowed.shape).astype(jnp.float32)]
    pallas_call x1, Pallas kernels: 6.86 us -> 5.63 us  [stay_attention(): pl.pallas_call(stay_kernel, out_shape=jax.ShapeDtypeStruct((HEADS, HD + 8...]
  transfers between devices with their start and end apart: 5 -> 5, of which waited for: 4 -> 3; matrix products, arithmetic and copies ran while one was open for 3% -> 2% of each run, Pallas kernels for 9% -> 10%
where the time goes in v3:
time: 109 us; the launch traced here: 108 us
  blocking collectives  44.1 us (40%)
  starting transfers between devices  35.7 us (33%)
  Pallas kernels  11.6 us (11%)
  waiting for transfers between devices  10.7 us (10%)
  local copies, waits for them, and re-layouts  4.16 us (4%)
    all_to_all x1, blocking collectives, local(): lax.all_to_all(out, SP, split_axis=0, concat_axis=0, tiled=True)  28.2 us
    all_to_all x1, starting transfers between devices, local(): box = lax.all_to_all(box, SP, split_axis=0, concat_axis=0, tiled=True)  17.4 us
    all_gather x1, blocking collectives, local(): gathered = lax.all_gather(box_out, ('x', 'c'), axis=0, tiled=True)  15.9 us
    ppermute x3, starting transfers between devices, swap(): return lax.ppermute(rows, 'z', [(i, i ^ bit) for i in range(8)])  14.5 us
    ppermute x3, waiting for transfers between devices, swap(): return lax.ppermute(rows, 'z', [(i, i ^ bit) for i in range(8)])  6.61 us
    pallas_call x1, Pallas kernels, stay_attention(): pl.pallas_call(stay_kernel, out_shape=jax.ShapeDtypeStruct((HEADS, HD + 8...  5.63 us
    all_to_all x1, waiting for transfers between devices, local(): box = lax.all_to_all(box, SP, split_axis=0, concat_axis=0, tiled=True)  4.04 us
    all_to_all x1, starting transfers between devices, local(): lax.all_to_all(stay.reshape(HEADS, 3 * HD, HD), SP, split_axis=0, concat_...  3.74 us
  transfers between devices with their start and end apart: 5, of which 3 were waited for; matrix products, arithmetic and copies ran while one was open for 2% of the time, Pallas kernels for 10%

profile of v3, /device:TPU:1, one launch (start us, length us, event | category | flops | bytes accessed | tf_op | source)
XLA Modules:
  0.0 108.4 jit_solution(14573494993525810161)
XLA Ops:
  0.6 0.0 copy-start
  0.6 0.9 copy-done
  1.5 0.7 copy_bitcast_fusion
  2.2 17.4 %all-to-all-start = ((bf16[16,24,128]{2,1,0:T(8,128)(2,1)}), bf16[16,24,128]{2,1,0:T(8,128)(2,1)S(1)}, u32[]{:S(2)}, u32[]{:S(2)}) async-start(bf16[16,24,128]{2,1,0:T(8,128)(2,1)} %copy_bitcast_fusion), calls=%async_computation | async-start | bytes 196608 | tf_op jit(solution)/shard_map/all_to_all | solution.py:239
  19.6 0.0 copy-start.1
  19.6 1.4 %copy-done.1 = bf16[1,128,3,2048]{3,1,2,0:T(8,128)(2,1)S(1)} copy-done((bf16[1,128,3,2048]{3,1,2,0:T(8,128)(2,1)S(1)}, bf16[1,128,3,2048]{3,1,2,0:T(8,128)(2,1)}, u32[]{:S(2)}) %copy-start.1) | copy-done | bytes 1572888
  21.0 0.0 copy-start.3
  21.0 0.7 copy-done.3
  21.7 2.4 %split_heads.1 = (bf16[16,3,128,128]{3,2,1,0:T(8,128)(2,1)}, f32[2,128,128]{2,1,0:T(8,128)S(1)}) custom-call(s32[128]{0:T(128)S(1)} %copy-done.3, bf16[3,128,2048]{2,1,0:T(8,128)(2,1)S(1)} %bitcast.41), custom_call_target="tpu_custom_call" | custom-call | tf_op jit(solution)/shard_map/split_heads/pallas_call | solution.py:149
  24.1 4.0 %all-to-all-done = bf16[16,24,128]{2,1,0:T(8,128)(2,1)S(1)} async-done(((bf16[16,24,128]{2,1,0:T(8,128)(2,1)}), bf16[16,24,128]{2,1,0:T(8,128)(2,1)S(1)}, u32[]{:S(2)}, u32[]{:S(2)}) %all-to-all-start) | async-done | bytes 98336 | tf_op jit(solution)/shard_map/all_to_all | solution.py:239
  28.2 0.0 copy-start.4
  28.2 3.7 %all-to-all-start.1 = ((bf16[16,384,128]{2,1,0:T(8,128)(2,1)}), bf16[16,384,128]{2,1,0:T(8,128)(2,1)S(1)}, u32[]{:S(2)}, u32[]{:S(2)}) async-start(bf16[16,384,128]{2,1,0:T(8,128)(2,1)} %bitcast.13), calls=%async_computation.1 | async-start | bytes 3145728 | tf_op jit(solution)/shard_map/all_to_all | solution.py:242
  31.9 0.0 copy-start.2
  31.9 0.2 fusion.10
  32.2 0.2 fusion.4
  32.4 0.2 fusion.1
  32.6 15.9 %all_gather.3 = bf16[2048,128]{1,0:T(8,128)(2,1)S(1)} all-gather(bf16[128,128]{1,0:T(8,128)(2,1)S(1)} %fusion.1), channel_id=1, replica_groups=mesh['x'=8,'z'=8,'y'=8,'c'=2] {'x','c'}, dimensions={0}, use_global_device_ids=true | all-gather | bytes 557056 | tf_op jit(solution)/shard_map/all_gather | solution.py:248
  48.5 0.0 copy-done.4
  48.5 1.1 %select_clips.1 = (bf16[8,64,128]{2,1,0:T(8,128)(2,1)S(1)}, bf16[8,64,128]{2,1,0:T(8,128)(2,1)S(1)}) custom-call(s32[128]{0:T(128)S(1)} %copy-done.4, bf16[16,2,64,128]{3,2,1,0:T(8,128)(2,1)S(1)} %bitcast.40), custom_call_target="tpu_custom_call" | custom-call | tf_op jit(solution)/shard_map/select_clips/pallas_call | solution.py:222
  49.7 1.9 %collective-permute-start = (bf16[8,64,128]{2,1,0:T(8,128)(2,1)S(1)}, bf16[8,64,128]{2,1,0:T(8,128)(2,1)S(1)}, u32[]{:S(2)}, u32[]{:S(2)}) collective-permute-start(bf16[8,64,128]{2,1,0:T(8,128)(2,1)S(1)} %get-tuple-element.26), channel_id=1, source_target_pairs={{0,16},{16,0},{32,48},{48,32},{64,80},{80,64},{96,112},{112,96},{1... | collective-permute-start | bytes 393224 | tf_op jit(solution)/shard_map/ppermute | solution.py:233
  51.6 0.5 broadcast.19
  52.1 0.0 copy-done.2
  52.1 0.7 reduce.3
  52.8 1.5 %stay_plan.1 = (s32[8]{0:T(128)S(1)}, s32[4]{0:T(128)S(1)}, s32[2048,128]{1,0:T(8,128)S(1)}) custom-call(s32[1,2048]{1,0:T(1,128)S(1)} %copy-done.2, s32[8,256]{1,0:T(8,128)S(1)} %reshape.34.clip_ref), custom_call_target="tpu_custom_call" | custom-call | flops 10000000 | bytes 1048576 | tf_op jit(solution)/shard_map/stay_plan/pallas_call | solution.py:100
  54.2 2.2 %collective-permute-done = bf16[8,64,128]{2,1,0:T(8,128)(2,1)S(1)} collective-permute-done((bf16[8,64,128]{2,1,0:T(8,128)(2,1)S(1)}, bf16[8,64,128]{2,1,0:T(8,128)(2,1)S(1)}, u32[]{:S(2)}, u32[]{:S(2)}) %collective-permute-start) | collective-permute-done | bytes 131104 | tf_op jit(solution)/shard_map/ppermute | solution.py:233
  56.5 3.4 %collective-permute-start.1 = (bf16[4,64,128]{2,1,0:T(8,128)(2,1)S(1)}, bf16[4,64,128]{2,1,0:T(8,128)(2,1)S(1)}, u32[]{:S(2)}, u32[]{:S(2)}) collective-permute-start(bf16[4,64,128]{2,1,0:T(8,128)(2,1)S(1)} %slice.32), channel_id=1, source_target_pairs={{0,32},{16,48},{32,0},{48,16},{64,96},{80,112},{96,64},{112,80},{1... | collective-permute-start | bytes 196616 | tf_op jit(solution)/shard_map/ppermute | solution.py:233
  59.9 4.4 %collective-permute-done.1 = bf16[4,64,128]{2,1,0:T(8,128)(2,1)S(1)} collective-permute-done((bf16[4,64,128]{2,1,0:T(8,128)(2,1)S(1)}, bf16[4,64,128]{2,1,0:T(8,128)(2,1)S(1)}, u32[]{:S(2)}, u32[]{:S(2)}) %collective-permute-start.1) | collective-permute-done | bytes 65568 | tf_op jit(solution)/shard_map/ppermute | solution.py:233
  64.3 9.2 %collective-permute-start.2 = (bf16[2,64,128]{2,1,0:T(8,128)(2,1)S(1)}, bf16[2,64,128]{2,1,0:T(8,128)(2,1)S(1)}, u32[]{:S(2)}, u32[]{:S(2)}) collective-permute-start(bf16[2,64,128]{2,1,0:T(8,128)(2,1)S(1)} %slice.33), channel_id=1, source_target_pairs={{0,64},{16,80},{32,96},{48,112},{64,0},{80,16},{96,32},{112,48},{1... | collective-permute-start | bytes 98312 | tf_op jit(solution)/shard_map/ppermute | solution.py:233
  73.5 0.0 all-to-all-done.1
  73.5 5.6 %stay_attention.1 = bf16[16,136,128]{2,1,0:T(8,128)(2,1)S(1)} custom-call(s32[8]{0:T(128)S(1)} %get-tuple-element.31.low_ref, s32[4]{0:T(128)S(1)} %get-tuple-element.32.pick_ref, bf16[16,3,128,128]{3,2,1,0:T(8,128)(2,1)S(1)} %bitcast.39, s32[8,1,256]{2,1,0:T(1,128)S(1)} %bitcast.42, s32[2048,128]{1,0:T(8,128)S(1)} %get-tuple-element.35.query_clip_ref), custom_call_target="tpu_custom_call" | custom-call | tf_op jit(solution)/shard_map/stay_attention/pallas_call | solution.py:118
  79.2 0.0 collective-permute-done.2
  79.2 28.2 %all_to_all.15.back_ref = bf16[16,136,128]{2,1,0:T(8,128)(2,1)S(1)} all-to-all(bf16[16,136,128]{2,1,0:T(8,128)(2,1)S(1)} %constant_dynamic-update-slice_fusion), channel_id=1, replica_groups=mesh['x'=8,'z'=8,'y'=8,'c'=2] {'y','c'}, dimensions={0} | all-to-all | bytes 1114112 | tf_op jit(solution)/shard_map/all_to_all | solution.py:262
  107.5 0.9 merge_heads.1
  (7 shorter events, 0.1 us)
Async XLA Ops:
  0.6 0.9 copy-start
  2.2 26.0 %all-to-all-start = ((bf16[16,24,128]{2,1,0:T(8,128)(2,1)}), bf16[16,24,128]{2,1,0:T(8,128)(2,1)S(1)}, u32[]{:S(2)}, u32[]{:S(2)}) async-start(bf16[16,24,128]{2,1,0:T(8,128)(2,1)} %copy_bitcast_fusion), calls=%async_computation | async-start | bytes 196608 | tf_op jit(solution)/shard_map/all_to_all | solution.py:239
  19.6 1.4 %copy-start.1 = (bf16[1,128,3,2048]{3,1,2,0:T(8,128)(2,1)S(1)}, bf16[1,128,3,2048]{3,1,2,0:T(8,128)(2,1)}, u32[]{:S(2)}) copy-start(bf16[1,128,3,2048]{3,1,2,0:T(8,128)(2,1)} %param.5) | copy-start | bytes 4718596
  21.0 0.7 copy-start.3
  28.2 20.3 %copy-start.4 = (s32[128]{0:T(128)S(1)}, s32[128]{0:T(128)}, u32[]{:S(2)}) copy-start(s32[128]{0:T(128)} %place_ref.1) | copy-start | bytes 1540
  28.2 45.4 %all-to-all-start.1 = ((bf16[16,384,128]{2,1,0:T(8,128)(2,1)}), bf16[16,384,128]{2,1,0:T(8,128)(2,1)S(1)}, u32[]{:S(2)}, u32[]{:S(2)}) async-start(bf16[16,384,128]{2,1,0:T(8,128)(2,1)} %bitcast.13), calls=%async_computation.1 | async-start | bytes 3145728 | tf_op jit(solution)/shard_map/all_to_all | solution.py:242
  31.9 20.2 %copy-start.2 = (s32[1,2048]{1,0:T(1,128)S(1)}, s32[1,2048]{1,0:T(1,128)}, u32[]{:S(2)}) copy-start(s32[1,2048]{1,0:T(1,128)} %edge_ref) | copy-start | bytes 24580
  49.7 6.8 %collective-permute-start = (bf16[8,64,128]{2,1,0:T(8,128)(2,1)S(1)}, bf16[8,64,128]{2,1,0:T(8,128)(2,1)S(1)}, u32[]{:S(2)}, u32[]{:S(2)}) collective-permute-start(bf16[8,64,128]{2,1,0:T(8,128)(2,1)S(1)} %get-tuple-element.26), channel_id=1, source_target_pairs={{0,16},{16,0},{32,48},{48,32},{64,80},{80,64},{96,112},{112,96},{1... | collective-permute-start | bytes 393224 | tf_op jit(solution)/shard_map/ppermute | solution.py:233
  56.5 7.7 %collective-permute-start.1 = (bf16[4,64,128]{2,1,0:T(8,128)(2,1)S(1)}, bf16[4,64,128]{2,1,0:T(8,128)(2,1)S(1)}, u32[]{:S(2)}, u32[]{:S(2)}) collective-permute-start(bf16[4,64,128]{2,1,0:T(8,128)(2,1)S(1)} %slice.32), channel_id=1, source_target_pairs={{0,32},{16,48},{32,0},{48,16},{64,96},{80,112},{96,64},{112,80},{1... | collective-permute-start | bytes 196616 | tf_op jit(solution)/shard_map/ppermute | solution.py:233
  64.3 14.9 %collective-permute-start.2 = (bf16[2,64,128]{2,1,0:T(8,128)(2,1)S(1)}, bf16[2,64,128]{2,1,0:T(8,128)(2,1)S(1)}, u32[]{:S(2)}, u32[]{:S(2)}) collective-permute-start(bf16[2,64,128]{2,1,0:T(8,128)(2,1)S(1)} %slice.33), channel_id=1, source_target_pairs={{0,64},{16,80},{32,96},{48,112},{64,0},{80,16},{96,32},{112,48},{1... | collective-permute-start | bytes 98312 | tf_op jit(solution)/shard_map/ppermute | solution.py:233

commit v4 on v3

--- a/solution.py
+++ b/solution.py
@@ -31,7 +31,7 @@
             product = lax.dot_general(
                 queries, keys, (((1,), (1,)), ((), ())), preferred_element_type=jnp.float32
             )
-            key_clip = key_clip_ref[low + j]
+            key_clip = key_clip_ref[:, pl.ds(pl.multiple_of((low + j) * ROWS, ROWS), ROWS)]
             for part in (slice(0, HD), slice(HD, 2 * HD)):
                 masked = jnp.where(query_clip == key_clip[:, part], product[:, part], -1e30)
                 peak = masked if peak is None else jnp.maximum(peak, masked)
@@ -90,13 +90,12 @@
         for index, low in zip((2 * pair, 2 * pair + 1), lows):
             low_ref[index] = jnp.minimum(low, BLOCKS - count)
     for index in range(BLOCKS):
-        row = jnp.broadcast_to(clip[index : index + 1], (HD, ROWS))
+        row = jnp.broadcast_to(clip[:, index * ROWS : (index + 1) * ROWS], (HD, ROWS))
         query_clip_ref[index * ROWS : (index + 1) * ROWS, :] = jnp.transpose(row)
 
 
 def stay_plan(clip):
     smem, vmem = pl.BlockSpec(memory_space=pltpu.SMEM), pl.BlockSpec(memory_space=pltpu.VMEM)
-    blocks = clip.reshape(BLOCKS, ROWS)
     low, pick, query_clip = pl.pallas_call(
         plan_kernel,
         out_shape=[
@@ -109,8 +108,8 @@
         compiler_params=pltpu.CompilerParams(vmem_limit_bytes=8 * 2**20),
         cost_estimate=pl.CostEstimate(flops=10**7, bytes_accessed=2**20, transcendentals=0),
         name="stay_plan",
-    )(clip, blocks)
-    return low, pick, blocks.reshape(BLOCKS, 1, ROWS), query_clip
+    )(clip, clip)
+    return low, pick, clip, query_clip
 
 
 def stay_attention(plan, rows):
@@ -161,7 +160,6 @@
             pl.BlockSpec((HEADS, 1, HD, HD), lambda t: (0, t, 0, 0)),
             pl.BlockSpec((2, 2 * HALF, 2 * HALF), lambda t: (0, 0, 0)),
         ],
-        compiler_params=pltpu.CompilerParams(vmem_limit_bytes=48 * 2**20),
         name="split_heads",
     )(out_len, rows)
 
@@ -201,29 +199,29 @@
     return with_layout_constraint(result, Layout(major_to_minor=(0, 1)))
 
 
-def select_kernel(place_ref, gathered_ref, keep_ref, send_ref):
+def select_kernel(place_ref, gathered_ref, *slot_refs):
     x, z, c = lax.axis_index("x"), lax.axis_index("z"), lax.axis_index("c")
-    keep_ref[...] = jnp.zeros_like(keep_ref)
-    send_ref[...] = jnp.zeros_like(send_ref)
+    for slot_ref in slot_refs:
+        slot_ref[...] = jnp.zeros_like(slot_ref)
     for source in range(16):
         place = place_ref[2 * ((source // 2) * 8 + z) + source % 2]
         far = (place // 2) % 8 ^ z
-        slot = (far // 2 % 2) * 4 + (far // 4) * 2 + place % 2
-        mine = place // 16 == x
-        for odd, slots_ref in enumerate((keep_ref, send_ref)):
-
-            @pl.when(mine & (far % 2 == odd))
-            def _(source=source, slot=slot, slots_ref=slots_ref):
-                slots_ref[slot] = gathered_ref[2 * (source // 2) + c, source % 2]
+        slot = (far // 4) * 2 + place % 2
+        near = jnp.where(place // 16 == x, far % 4, -1)
+        for u, slot_ref in enumerate(slot_refs):
+
+            @pl.when(near == u)
+            def _(source=source, slot=slot, slot_ref=slot_ref):
+                slot_ref[slot] = gathered_ref[2 * (source // 2) + c, source % 2]
 
 
 def select(place, gathered):
     smem, vmem = pl.BlockSpec(memory_space=pltpu.SMEM), pl.BlockSpec(memory_space=pltpu.VMEM)
     return pl.pallas_call(
         select_kernel,
-        out_shape=[jax.ShapeDtypeStruct((8, HALF, HD), jnp.bfloat16)] * 2,
+        out_shape=[jax.ShapeDtypeStruct((4, HALF, HD), jnp.bfloat16)] * 4,
         in_specs=[smem, vmem],
-        out_specs=[vmem] * 2,
+        out_specs=[vmem] * 4,
         compiler_params=pltpu.CompilerParams(vmem_limit_bytes=4 * 2**20),
         name="select_clips",
     )(place, gathered)
@@ -246,12 +244,11 @@
     box_out = box_attention(masks, box.reshape(HEADS, 3, 8, HD))
 
     gathered = lax.all_gather(box_out, ("x", "c"), axis=0, tiled=True)
-    keep, send = select(out_place, gathered.reshape(16, 2, HALF, HD))
-    send, clip = lax.optimization_barrier((send, stay_clip))
-    came, plan = lax.optimization_barrier((swap(send, 1), stay_plan(clip)))
-    slots = keep + came
-    came = swap(slots[4:], 2)
-    slots = slots[:4] + came
+    slots = select(out_place, gathered.reshape(16, 2, HALF, HD))
+    slots, clip = lax.optimization_barrier((slots, stay_clip))
+    came = swap(slots[3], 3), swap(slots[2], 2), swap(slots[1], 1)
+    came, plan = lax.optimization_barrier((came, stay_plan(clip)))
+    slots = slots[0] + came[0] + came[1] + came[2]
     came = swap(slots[2:], 4)
 
     out = stay_attention(plan, stay.reshape(HEADS, 3, HD, HD))

time: 109 us -> 107 us (0.982)
  starting transfers between devices: 35.7 us -> 42.1 us
  waiting for transfers between devices: 10.7 us -> 6.61 us
  local copies, waits for them, and re-layouts: 4.16 us -> 1.58 us
  blocking collectives: 44.1 us -> 42.1 us
  Pallas kernels: 11.6 us -> 13 us
    ppermute x3 -> x4, starting transfers between devices: 14.5 us -> 20.9 us  [swap(): return lax.ppermute(rows, 'z', [(i, i ^ bit) for i in range(8)])]
    ppermute x3 -> x4, waiting for transfers between devices: 6.61 us -> 1.65 us  [swap(): return lax.ppermute(rows, 'z', [(i, i ^ bit) for i in range(8)])]
    unnamed x10 -> x8, local copies, waits for them, and re-layouts: 2.96 us -> 0.9 us
    all_to_all x1, blocking collectives: 28.2 us -> 26.2 us  [local(): lax.all_to_all(out, SP, split_axis=0, concat_axis=0, tiled=True)]
    pallas_call x1, Pallas kernels: 2.41 us -> 3.55 us  [split_heads(): pl.pallas_call(split_kernel, grid=(3,), out_shape=[jax.ShapeDtypeStruct((...]
  transfers between devices with their start and end apart: 5 -> 6, of which waited for: 3 -> 2; matrix products, arithmetic and copies ran while one was open for 2% -> 1% of each run, Pallas kernels for 10% -> 11%
where the time goes in v4:
time: 107 us
  starting transfers between devices  42.1 us (39%)
  blocking collectives  42.1 us (39%)
  Pallas kernels  13 us (12%)
  waiting for transfers between devices  6.61 us (6%)
  local copies, waits for them, and re-layouts  1.58 us (1%)
    all_to_all x1, blocking collectives, local(): lax.all_to_all(out, SP, split_axis=0, concat_axis=0, tiled=True)  26.2 us
    ppermute x4, starting transfers between devices, swap(): return lax.ppermute(rows, 'z', [(i, i ^ bit) for i in range(8)])  20.9 us
    all_to_all x1, starting transfers between devices, local(): box = lax.all_to_all(box, SP, split_axis=0, concat_axis=0, tiled=True)  17.4 us
    all_gather x1, blocking collectives, local(): gathered = lax.all_gather(box_out, ('x', 'c'), axis=0, tiled=True)  15.9 us
    pallas_call x1, Pallas kernels, stay_attention(): pl.pallas_call(stay_kernel, out_shape=jax.ShapeDtypeStruct((HEADS, HD + 8...  5.72 us
    all_to_all x1, waiting for transfers between devices, local(): box = lax.all_to_all(box, SP, split_axis=0, concat_axis=0, tiled=True)  4.96 us
    all_to_all x1, starting transfers between devices, local(): lax.all_to_all(stay.reshape(HEADS, 3 * HD, HD), SP, split_axis=0, concat_...  3.74 us
    pallas_call x1, Pallas kernels, split_heads(): pl.pallas_call(split_kernel, grid=(3,), out_shape=[jax.ShapeDtypeStruct((...  3.55 us
  transfers between devices with their start and end apart: 6, of which 2 were waited for; matrix products, arithmetic and copies ran while one was open for 1% of the time, Pallas kernels for 11%

profile of v4, /device:TPU:1, one launch (start us, length us, event | category | flops | bytes accessed | tf_op | source)
XLA Modules:
  0.0 106.9 jit_solution(15702327480852268090)
XLA Ops:
  0.6 0.0 copy-start
  0.6 0.9 copy-done
  1.5 0.7 copy_bitcast_fusion
  2.2 17.4 %all-to-all-start = ((bf16[16,24,128]{2,1,0:T(8,128)(2,1)}), bf16[16,24,128]{2,1,0:T(8,128)(2,1)S(1)}, u32[]{:S(2)}, u32[]{:S(2)}) async-start(bf16[16,24,128]{2,1,0:T(8,128)(2,1)} %copy_bitcast_fusion), calls=%async_computation | async-start | bytes 196608 | tf_op jit(solution)/shard_map/all_to_all | solution.py:237
  19.6 3.6 %split_heads.1 = (bf16[16,3,128,128]{3,2,1,0:T(8,128)(2,1)}, f32[2,128,128]{2,1,0:T(8,128)}) custom-call(s32[128]{0:T(128)} %length_ref.1, bf16[3,128,2048]{2,1,0:T(8,128)(2,1)} %bitcast.40), custom_call_target="tpu_custom_call" | custom-call | tf_op jit(solution)/shard_map/split_heads/pallas_call | solution.py:148
  23.2 5.0 %all-to-all-done = bf16[16,24,128]{2,1,0:T(8,128)(2,1)S(1)} async-done(((bf16[16,24,128]{2,1,0:T(8,128)(2,1)}), bf16[16,24,128]{2,1,0:T(8,128)(2,1)S(1)}, u32[]{:S(2)}, u32[]{:S(2)}) %all-to-all-start) | async-done | bytes 98336 | tf_op jit(solution)/shard_map/all_to_all | solution.py:237
  28.1 0.0 copy-start.3
  28.2 0.0 copy-start.2
  28.2 3.7 %all-to-all-start.1 = ((bf16[16,384,128]{2,1,0:T(8,128)(2,1)}), bf16[16,384,128]{2,1,0:T(8,128)(2,1)S(1)}, u32[]{:S(2)}, u32[]{:S(2)}) async-start(bf16[16,384,128]{2,1,0:T(8,128)(2,1)} %bitcast.41), calls=%async_computation.1 | async-start | bytes 3145728 | tf_op jit(solution)/shard_map/all_to_all | solution.py:240
  31.9 0.0 copy-start.1
  31.9 0.0 copy-done.3
  31.9 0.2 fusion.10
  32.2 0.2 fusion.4
  32.4 0.2 fusion.1
  32.6 15.9 %all_gather.3 = bf16[2048,128]{1,0:T(8,128)(2,1)S(1)} all-gather(bf16[128,128]{1,0:T(8,128)(2,1)S(1)} %fusion.1), channel_id=1, replica_groups=mesh['x'=8,'z'=8,'y'=8,'c'=2] {'x','c'}, dimensions={0}, use_global_device_ids=true | all-gather | bytes 557056 | tf_op jit(solution)/shard_map/all_gather | solution.py:246
  48.5 0.0 copy-done.2
  48.5 1.2 %select_clips.1 = (bf16[4,64,128]{2,1,0:T(8,128)(2,1)S(1)}, bf16[4,64,128]{2,1,0:T(8,128)(2,1)S(1)}, bf16[4,64,128]{2,1,0:T(8,128)(2,1)S(1)}, bf16[4,64,128]{2,1,0:T(8,128)(2,1)S(1)}) custom-call(s32[128]{0:T(128)S(1)} %copy-done.2, bf16[16,2,64,128]{3,2,1,0:T(8,128)(2,1)S(1)} %bitcast.39), custom_call_target="tpu_custom_call" | custom-call | tf_op jit(solution)/shard_map/select_clips/pallas_call | solution.py:220
  49.7 4.3 %collective-permute-start = (bf16[4,64,128]{2,1,0:T(8,128)(2,1)S(1)}, bf16[4,64,128]{2,1,0:T(8,128)(2,1)S(1)}, u32[]{:S(2)}, u32[]{:S(2)}) collective-permute-start(bf16[4,64,128]{2,1,0:T(8,128)(2,1)S(1)} %get-tuple-element.36), channel_id=1, source_target_pairs={{0,48},{16,32},{32,16},{48,0},{64,112},{80,96},{96,80},{112,64},{1... | collective-permute-start | bytes 196616 | tf_op jit(solution)/shard_map/ppermute | solution.py:231
  54.1 1.9 %collective-permute-start.1 = (bf16[4,64,128]{2,1,0:T(8,128)(2,1)S(1)}, bf16[4,64,128]{2,1,0:T(8,128)(2,1)S(1)}, u32[]{:S(2)}, u32[]{:S(2)}) collective-permute-start(bf16[4,64,128]{2,1,0:T(8,128)(2,1)S(1)} %get-tuple-element.37), channel_id=1, source_target_pairs={{0,32},{16,48},{32,0},{48,16},{64,96},{80,112},{96,64},{112,80},{1... | collective-permute-start | bytes 196616 | tf_op jit(solution)/shard_map/ppermute | solution.py:231
  56.0 3.0 %collective-permute-start.2 = (bf16[4,64,128]{2,1,0:T(8,128)(2,1)S(1)}, bf16[4,64,128]{2,1,0:T(8,128)(2,1)S(1)}, u32[]{:S(2)}, u32[]{:S(2)}) collective-permute-start(bf16[4,64,128]{2,1,0:T(8,128)(2,1)S(1)} %get-tuple-element.38), channel_id=1, source_target_pairs={{0,16},{16,0},{32,48},{48,32},{64,80},{80,64},{96,112},{112,96},{1... | collective-permute-start | bytes 196616 | tf_op jit(solution)/shard_map/ppermute | solution.py:231
  59.0 0.0 copy-done.1
  59.0 1.5 %stay_plan.1 = (s32[8]{0:T(128)S(1)}, s32[4]{0:T(128)S(1)}, s32[2048,128]{1,0:T(8,128)S(1)}) custom-call(s32[1,2048]{1,0:T(1,128)S(1)} %copy-done.1, s32[1,2048]{1,0:T(1,128)S(1)} %copy-done.1), custom_call_target="tpu_custom_call" | custom-call | flops 10000000 | bytes 1048576 | tf_op jit(solution)/shard_map/stay_plan/pallas_call | solution.py:99
  60.6 0.0 collective-permute-done
  60.6 0.0 collective-permute-done.1
  60.6 1.6 %collective-permute-done.2 = bf16[4,64,128]{2,1,0:T(8,128)(2,1)S(1)} collective-permute-done((bf16[4,64,128]{2,1,0:T(8,128)(2,1)S(1)}, bf16[4,64,128]{2,1,0:T(8,128)(2,1)S(1)}, u32[]{:S(2)}, u32[]{:S(2)}) %collective-permute-start.2) | collective-permute-done | bytes 65568 | tf_op jit(solution)/shard_map/ppermute | solution.py:231
  62.3 11.6 %collective-permute-start.3 = (bf16[2,64,128]{2,1,0:T(8,128)(2,1)S(1)}, bf16[2,64,128]{2,1,0:T(8,128)(2,1)S(1)}, u32[]{:S(2)}, u32[]{:S(2)}) collective-permute-start(bf16[2,64,128]{2,1,0:T(8,128)(2,1)S(1)} %slice.23), channel_id=1, source_target_pairs={{0,64},{16,80},{32,96},{48,112},{64,0},{80,16},{96,32},{112,48},{1... | collective-permute-start | bytes 98312 | tf_op jit(solution)/shard_map/ppermute | solution.py:231
  73.9 0.0 all-to-all-done.1
  73.9 5.7 %stay_attention.1 = bf16[16,136,128]{2,1,0:T(8,128)(2,1)S(1)} custom-call(s32[8]{0:T(128)S(1)} %get-tuple-element.43.low_ref, s32[4]{0:T(128)S(1)} %get-tuple-element.44.pick_ref, bf16[16,3,128,128]{3,2,1,0:T(8,128)(2,1)S(1)} %bitcast.38, s32[1,2048]{1,0:T(1,128)S(1)} %copy-done.1, s32[2048,128]{1,0:T(8,128)S(1)} %get-tuple-element.47.query_clip_ref), custom_call_target="tpu_custom_call" | custom-call | tf_op jit(solution)/shard_map/stay_attention/pallas_call | solution.py:117
  79.6 0.0 collective-permute-done.3
  79.7 26.2 %all_to_all.15.back_ref = bf16[16,136,128]{2,1,0:T(8,128)(2,1)S(1)} all-to-all(bf16[16,136,128]{2,1,0:T(8,128)(2,1)S(1)} %constant_dynamic-update-slice_fusion), channel_id=1, replica_groups=mesh['x'=8,'z'=8,'y'=8,'c'=2] {'y','c'}, dimensions={0} | all-to-all | bytes 1114112 | tf_op jit(solution)/shard_map/all_to_all | solution.py:259
  105.9 0.9 merge_heads.1
  (4 shorter events, 0.0 us)
Async XLA Ops:
  0.6 0.9 copy-start
  2.2 26.0 %all-to-all-start = ((bf16[16,24,128]{2,1,0:T(8,128)(2,1)}), bf16[16,24,128]{2,1,0:T(8,128)(2,1)S(1)}, u32[]{:S(2)}, u32[]{:S(2)}) async-start(bf16[16,24,128]{2,1,0:T(8,128)(2,1)} %copy_bitcast_fusion), calls=%async_computation | async-start | bytes 196608 | tf_op jit(solution)/shard_map/all_to_all | solution.py:237
  28.1 3.8 %copy-start.3 = (f32[2,128,128]{2,1,0:T(8,128)S(1)}, f32[2,128,128]{2,1,0:T(8,128)}, u32[]{:S(2)}) copy-start(f32[2,128,128]{2,1,0:T(8,128)} %get-tuple-element.29) | copy-start | bytes 393220
  28.2 20.4 %copy-start.2 = (s32[128]{0:T(128)S(1)}, s32[128]{0:T(128)}, u32[]{:S(2)}) copy-start(s32[128]{0:T(128)} %place_ref.1) | copy-start | bytes 1540
  28.2 45.7 %all-to-all-start.1 = ((bf16[16,384,128]{2,1,0:T(8,128)(2,1)}), bf16[16,384,128]{2,1,0:T(8,128)(2,1)S(1)}, u32[]{:S(2)}, u32[]{:S(2)}) async-start(bf16[16,384,128]{2,1,0:T(8,128)(2,1)} %bitcast.41), calls=%async_computation.1 | async-start | bytes 3145728 | tf_op jit(solution)/shard_map/all_to_all | solution.py:240
  31.9 27.1 %copy-start.1 = (s32[1,2048]{1,0:T(1,128)S(1)}, s32[1,2048]{1,0:T(1,128)}, u32[]{:S(2)}) copy-start(s32[1,2048]{1,0:T(1,128)} %key_clip_ref) | copy-start | bytes 24580
  49.7 10.9 %collective-permute-start = (bf16[4,64,128]{2,1,0:T(8,128)(2,1)S(1)}, bf16[4,64,128]{2,1,0:T(8,128)(2,1)S(1)}, u32[]{:S(2)}, u32[]{:S(2)}) collective-permute-start(bf16[4,64,128]{2,1,0:T(8,128)(2,1)S(1)} %get-tuple-element.36), channel_id=1, source_target_pairs={{0,48},{16,32},{32,16},{48,0},{64,112},{80,96},{96,80},{112,64},{1... | collective-permute-start | bytes 196616 | tf_op jit(solution)/shard_map/ppermute | solution.py:231
  54.1 6.5 %collective-permute-start.1 = (bf16[4,64,128]{2,1,0:T(8,128)(2,1)S(1)}, bf16[4,64,128]{2,1,0:T(8,128)(2,1)S(1)}, u32[]{:S(2)}, u32[]{:S(2)}) collective-permute-start(bf16[4,64,128]{2,1,0:T(8,128)(2,1)S(1)} %get-tuple-element.37), channel_id=1, source_target_pairs={{0,32},{16,48},{32,0},{48,16},{64,96},{80,112},{96,64},{112,80},{1... | collective-permute-start | bytes 196616 | tf_op jit(solution)/shard_map/ppermute | solution.py:231
  56.0 6.3 %collective-permute-start.2 = (bf16[4,64,128]{2,1,0:T(8,128)(2,1)S(1)}, bf16[4,64,128]{2,1,0:T(8,128)(2,1)S(1)}, u32[]{:S(2)}, u32[]{:S(2)}) collective-permute-start(bf16[4,64,128]{2,1,0:T(8,128)(2,1)S(1)} %get-tuple-element.38), channel_id=1, source_target_pairs={{0,16},{16,0},{32,48},{48,32},{64,80},{80,64},{96,112},{112,96},{1... | collective-permute-start | bytes 196616 | tf_op jit(solution)/shard_map/ppermute | solution.py:231
  62.3 17.4 %collective-permute-start.3 = (bf16[2,64,128]{2,1,0:T(8,128)(2,1)S(1)}, bf16[2,64,128]{2,1,0:T(8,128)(2,1)S(1)}, u32[]{:S(2)}, u32[]{:S(2)}) collective-permute-start(bf16[2,64,128]{2,1,0:T(8,128)(2,1)S(1)} %slice.23), channel_id=1, source_target_pairs={{0,64},{16,80},{32,96},{48,112},{64,0},{80,16},{96,32},{112,48},{1... | collective-permute-start | bytes 98312 | tf_op jit(solution)/shard_map/ppermute | solution.py:231

commit v5 on v4

--- a/solution.py
+++ b/solution.py
@@ -206,8 +206,8 @@
     for source in range(16):
         place = place_ref[2 * ((source // 2) * 8 + z) + source % 2]
         far = (place // 2) % 8 ^ z
-        slot = (far // 4) * 2 + place % 2
-        near = jnp.where(place // 16 == x, far % 4, -1)
+        slot = (far // 2 % 2) * 2 + place % 2
+        near = jnp.where(place // 16 == x, (far // 4) * 2 + far % 2, -1)
         for u, slot_ref in enumerate(slot_refs):
 
             @pl.when(near == u)
@@ -246,10 +246,10 @@
     gathered = lax.all_gather(box_out, ("x", "c"), axis=0, tiled=True)
     slots = select(out_place, gathered.reshape(16, 2, HALF, HD))
     slots, clip = lax.optimization_barrier((slots, stay_clip))
-    came = swap(slots[3], 3), swap(slots[2], 2), swap(slots[1], 1)
+    came = swap(slots[2], 4), swap(slots[3], 5), swap(slots[1], 1)
     came, plan = lax.optimization_barrier((came, stay_plan(clip)))
     slots = slots[0] + came[0] + came[1] + came[2]
-    came = swap(slots[2:], 4)
+    came = swap(slots[2:], 2)
 
     out = stay_attention(plan, stay.reshape(HEADS, 3, HD, HD))
     out, slots = lax.optimization_barrier((out, slots))

time: 107 us -> 106 us (level)
  starting transfers between devices: 42.1 us -> 39.9 us
  waiting for transfers between devices: 6.61 us -> 8.36 us
  Pallas kernels: 13 us -> 11.5 us
    ppermute x4, starting transfers between devices: 20.9 us -> 18.8 us  [swap(): return lax.ppermute(rows, 'z', [(i, i ^ bit) for i in range(8)])]
    ppermute x4, waiting for transfers between devices: 1.65 us -> 3.39 us  [swap(): return lax.ppermute(rows, 'z', [(i, i ^ bit) for i in range(8)])]
    pallas_call x1, Pallas kernels: 5.72 us -> 4.15 us  [stay_attention(): pl.pallas_call(stay_kernel, out_shape=jax.ShapeDtypeStruct((HEADS, HD + 8...]
  transfers between devices with their start and end apart: 6 -> 6, of which waited for: 2 -> 3; matrix products, arithmetic and copies ran while one was open for 1% -> 1% of each run, Pallas kernels for 11% -> 10%
where the time goes in v5:
time: 106 us; the launch traced here: 105 us
  blocking collectives  42 us (40%)
  starting transfers between devices  39.9 us (38%)
  Pallas kernels  11.5 us (11%)
  waiting for transfers between devices  8.36 us (8%)
  local copies, waits for them, and re-layouts  1.58 us (1%)
    all_to_all x1, blocking collectives, local(): lax.all_to_all(out, SP, split_axis=0, concat_axis=0, tiled=True)  26.1 us
    ppermute x4, starting transfers between devices, swap(): return lax.ppermute(rows, 'z', [(i, i ^ bit) for i in range(8)])  18.8 us
    all_to_all x1, starting transfers between devices, local(): box = lax.all_to_all(box, SP, split_axis=0, concat_axis=0, tiled=True)  17.4 us
    all_gather x1, blocking collectives, local(): gathered = lax.all_gather(box_out, ('x', 'c'), axis=0, tiled=True)  15.9 us
    all_to_all x1, waiting for transfers between devices, local(): box = lax.all_to_all(box, SP, split_axis=0, concat_axis=0, tiled=True)  4.96 us
    pallas_call x1, Pallas kernels, stay_attention(): pl.pallas_call(stay_kernel, out_shape=jax.ShapeDtypeStruct((HEADS, HD + 8...  4.15 us
    all_to_all x1, starting transfers between devices, local(): lax.all_to_all(stay.reshape(HEADS, 3 * HD, HD), SP, split_axis=0, concat_...  3.74 us
    pallas_call x1, Pallas kernels, split_heads(): pl.pallas_call(split_kernel, grid=(3,), out_shape=[jax.ShapeDtypeStruct((...  3.55 us
  transfers between devices with their start and end apart: 6, of which 3 were waited for; matrix products, arithmetic and copies ran while one was open for 1% of the time, Pallas kernels for 10%

profile of v5, /device:TPU:1, one launch (start us, length us, event | category | flops | bytes accessed | tf_op | source)
XLA Modules:
  0.0 104.8 jit_solution(1255870718582711295)
XLA Ops:
  0.6 0.0 copy-start
  0.6 0.9 copy-done
  1.5 0.7 copy_bitcast_fusion
  2.2 17.4 %all-to-all-start = ((bf16[16,24,128]{2,1,0:T(8,128)(2,1)}), bf16[16,24,128]{2,1,0:T(8,128)(2,1)S(1)}, u32[]{:S(2)}, u32[]{:S(2)}) async-start(bf16[16,24,128]{2,1,0:T(8,128)(2,1)} %copy_bitcast_fusion), calls=%async_computation | async-start | bytes 196608 | tf_op jit(solution)/shard_map/all_to_all | solution.py:237
  19.6 3.6 %split_heads.1 = (bf16[16,3,128,128]{3,2,1,0:T(8,128)(2,1)}, f32[2,128,128]{2,1,0:T(8,128)}) custom-call(s32[128]{0:T(128)} %length_ref.1, bf16[3,128,2048]{2,1,0:T(8,128)(2,1)} %bitcast.40), custom_call_target="tpu_custom_call" | custom-call | tf_op jit(solution)/shard_map/split_heads/pallas_call | solution.py:148
  23.2 5.0 %all-to-all-done = bf16[16,24,128]{2,1,0:T(8,128)(2,1)S(1)} async-done(((bf16[16,24,128]{2,1,0:T(8,128)(2,1)}), bf16[16,24,128]{2,1,0:T(8,128)(2,1)S(1)}, u32[]{:S(2)}, u32[]{:S(2)}) %all-to-all-start) | async-done | bytes 98336 | tf_op jit(solution)/shard_map/all_to_all | solution.py:237
  28.1 0.0 copy-start.3
  28.2 0.0 copy-start.2
  28.2 3.7 %all-to-all-start.1 = ((bf16[16,384,128]{2,1,0:T(8,128)(2,1)}), bf16[16,384,128]{2,1,0:T(8,128)(2,1)S(1)}, u32[]{:S(2)}, u32[]{:S(2)}) async-start(bf16[16,384,128]{2,1,0:T(8,128)(2,1)} %bitcast.41), calls=%async_computation.1 | async-start | bytes 3145728 | tf_op jit(solution)/shard_map/all_to_all | solution.py:240
  31.9 0.0 copy-start.1
  31.9 0.0 copy-done.3
  31.9 0.2 fusion.10
  32.2 0.2 fusion.4
  32.4 0.2 fusion.1
  32.6 15.9 %all_gather.3 = bf16[2048,128]{1,0:T(8,128)(2,1)S(1)} all-gather(bf16[128,128]{1,0:T(8,128)(2,1)S(1)} %fusion.1), channel_id=1, replica_groups=mesh['x'=8,'z'=8,'y'=8,'c'=2] {'x','c'}, dimensions={0}, use_global_device_ids=true | all-gather | bytes 557056 | tf_op jit(solution)/shard_map/all_gather | solution.py:246
  48.5 0.0 copy-done.2
  48.5 1.3 %select_clips.1 = (bf16[4,64,128]{2,1,0:T(8,128)(2,1)S(1)}, bf16[4,64,128]{2,1,0:T(8,128)(2,1)S(1)}, bf16[4,64,128]{2,1,0:T(8,128)(2,1)S(1)}, bf16[4,64,128]{2,1,0:T(8,128)(2,1)S(1)}) custom-call(s32[128]{0:T(128)S(1)} %copy-done.2, bf16[16,2,64,128]{3,2,1,0:T(8,128)(2,1)S(1)} %bitcast.39), custom_call_target="tpu_custom_call" | custom-call | tf_op jit(solution)/shard_map/select_clips/pallas_call | solution.py:220
  49.8 8.3 %collective-permute-start = (bf16[4,64,128]{2,1,0:T(8,128)(2,1)S(1)}, bf16[4,64,128]{2,1,0:T(8,128)(2,1)S(1)}, u32[]{:S(2)}, u32[]{:S(2)}) collective-permute-start(bf16[4,64,128]{2,1,0:T(8,128)(2,1)S(1)} %get-tuple-element.36), channel_id=1, source_target_pairs={{0,64},{16,80},{32,96},{48,112},{64,0},{80,16},{96,32},{112,48},{1... | collective-permute-start | bytes 196616 | tf_op jit(solution)/shard_map/ppermute | solution.py:231
  58.1 2.8 %collective-permute-start.1 = (bf16[4,64,128]{2,1,0:T(8,128)(2,1)S(1)}, bf16[4,64,128]{2,1,0:T(8,128)(2,1)S(1)}, u32[]{:S(2)}, u32[]{:S(2)}) collective-permute-start(bf16[4,64,128]{2,1,0:T(8,128)(2,1)S(1)} %get-tuple-element.37), channel_id=1, source_target_pairs={{0,80},{16,64},{32,112},{48,96},{64,16},{80,0},{96,48},{112,32},{1... | collective-permute-start | bytes 196616 | tf_op jit(solution)/shard_map/ppermute | solution.py:231
  60.9 3.1 %collective-permute-start.2 = (bf16[4,64,128]{2,1,0:T(8,128)(2,1)S(1)}, bf16[4,64,128]{2,1,0:T(8,128)(2,1)S(1)}, u32[]{:S(2)}, u32[]{:S(2)}) collective-permute-start(bf16[4,64,128]{2,1,0:T(8,128)(2,1)S(1)} %get-tuple-element.38), channel_id=1, source_target_pairs={{0,16},{16,0},{32,48},{48,32},{64,80},{80,64},{96,112},{112,96},{1... | collective-permute-start | bytes 196616 | tf_op jit(solution)/shard_map/ppermute | solution.py:231
  64.0 0.0 copy-done.1
  64.0 1.5 %stay_plan.1 = (s32[8]{0:T(128)S(1)}, s32[4]{0:T(128)S(1)}, s32[2048,128]{1,0:T(8,128)S(1)}) custom-call(s32[1,2048]{1,0:T(1,128)S(1)} %copy-done.1, s32[1,2048]{1,0:T(1,128)S(1)} %copy-done.1), custom_call_target="tpu_custom_call" | custom-call | flops 10000000 | bytes 1048576 | tf_op jit(solution)/shard_map/stay_plan/pallas_call | solution.py:99
  65.6 0.0 collective-permute-done
  65.6 2.1 %collective-permute-done.1 = bf16[4,64,128]{2,1,0:T(8,128)(2,1)S(1)} collective-permute-done((bf16[4,64,128]{2,1,0:T(8,128)(2,1)S(1)}, bf16[4,64,128]{2,1,0:T(8,128)(2,1)S(1)}, u32[]{:S(2)}, u32[]{:S(2)}) %collective-permute-start.1) | collective-permute-done | bytes 65568 | tf_op jit(solution)/shard_map/ppermute | solution.py:231
  67.7 1.3 %collective-permute-done.2 = bf16[4,64,128]{2,1,0:T(8,128)(2,1)S(1)} collective-permute-done((bf16[4,64,128]{2,1,0:T(8,128)(2,1)S(1)}, bf16[4,64,128]{2,1,0:T(8,128)(2,1)S(1)}, u32[]{:S(2)}, u32[]{:S(2)}) %collective-permute-start.2) | collective-permute-done | bytes 65568 | tf_op jit(solution)/shard_map/ppermute | solution.py:231
  69.0 4.6 %collective-permute-start.3 = (bf16[2,64,128]{2,1,0:T(8,128)(2,1)S(1)}, bf16[2,64,128]{2,1,0:T(8,128)(2,1)S(1)}, u32[]{:S(2)}, u32[]{:S(2)}) collective-permute-start(bf16[2,64,128]{2,1,0:T(8,128)(2,1)S(1)} %slice.23), channel_id=1, source_target_pairs={{0,32},{16,48},{32,0},{48,16},{64,96},{80,112},{96,64},{112,80},{1... | collective-permute-start | bytes 98312 | tf_op jit(solution)/shard_map/ppermute | solution.py:231
  73.6 0.0 all-to-all-done.1
  73.6 4.2 %stay_attention.1 = bf16[16,136,128]{2,1,0:T(8,128)(2,1)S(1)} custom-call(s32[8]{0:T(128)S(1)} %get-tuple-element.43.low_ref, s32[4]{0:T(128)S(1)} %get-tuple-element.44.pick_ref, bf16[16,3,128,128]{3,2,1,0:T(8,128)(2,1)S(1)} %bitcast.38, s32[1,2048]{1,0:T(1,128)S(1)} %copy-done.1, s32[2048,128]{1,0:T(8,128)S(1)} %get-tuple-element.47.query_clip_ref), custom_call_target="tpu_custom_call" | custom-call | tf_op jit(solution)/shard_map/stay_attention/pallas_call | solution.py:117
  77.8 0.0 collective-permute-done.3
  77.8 26.1 %all_to_all.15.back_ref = bf16[16,136,128]{2,1,0:T(8,128)(2,1)S(1)} all-to-all(bf16[16,136,128]{2,1,0:T(8,128)(2,1)S(1)} %constant_dynamic-update-slice_fusion), channel_id=1, replica_groups=mesh['x'=8,'z'=8,'y'=8,'c'=2] {'y','c'}, dimensions={0} | all-to-all | bytes 1114112 | tf_op jit(solution)/shard_map/all_to_all | solution.py:259
  103.9 0.9 merge_heads.1
  (4 shorter events, 0.0 us)
Async XLA Ops:
  0.6 0.9 copy-start
  2.2 26.0 %all-to-all-start = ((bf16[16,24,128]{2,1,0:T(8,128)(2,1)}), bf16[16,24,128]{2,1,0:T(8,128)(2,1)S(1)}, u32[]{:S(2)}, u32[]{:S(2)}) async-start(bf16[16,24,128]{2,1,0:T(8,128)(2,1)} %copy_bitcast_fusion), calls=%async_computation | async-start | bytes 196608 | tf_op jit(solution)/shard_map/all_to_all | solution.py:237
  28.1 3.8 %copy-start.3 = (f32[2,128,128]{2,1,0:T(8,128)S(1)}, f32[2,128,128]{2,1,0:T(8,128)}, u32[]{:S(2)}) copy-start(f32[2,128,128]{2,1,0:T(8,128)} %get-tuple-element.29) | copy-start | bytes 393220
  28.2 20.4 %copy-start.2 = (s32[128]{0:T(128)S(1)}, s32[128]{0:T(128)}, u32[]{:S(2)}) copy-start(s32[128]{0:T(128)} %place_ref.1) | copy-start | bytes 1540
  28.2 45.4 %all-to-all-start.1 = ((bf16[16,384,128]{2,1,0:T(8,128)(2,1)}), bf16[16,384,128]{2,1,0:T(8,128)(2,1)S(1)}, u32[]{:S(2)}, u32[]{:S(2)}) async-start(bf16[16,384,128]{2,1,0:T(8,128)(2,1)} %bitcast.41), calls=%async_computation.1 | async-start | bytes 3145728 | tf_op jit(solution)/shard_map/all_to_all | solution.py:240
  31.9 32.1 %copy-start.1 = (s32[1,2048]{1,0:T(1,128)S(1)}, s32[1,2048]{1,0:T(1,128)}, u32[]{:S(2)}) copy-start(s32[1,2048]{1,0:T(1,128)} %key_clip_ref) | copy-start | bytes 24580
  49.8 15.8 %collective-permute-start = (bf16[4,64,128]{2,1,0:T(8,128)(2,1)S(1)}, bf16[4,64,128]{2,1,0:T(8,128)(2,1)S(1)}, u32[]{:S(2)}, u32[]{:S(2)}) collective-permute-start(bf16[4,64,128]{2,1,0:T(8,128)(2,1)S(1)} %get-tuple-element.36), channel_id=1, source_target_pairs={{0,64},{16,80},{32,96},{48,112},{64,0},{80,16},{96,32},{112,48},{1... | collective-permute-start | bytes 196616 | tf_op jit(solution)/shard_map/ppermute | solution.py:231
  58.1 9.6 %collective-permute-start.1 = (bf16[4,64,128]{2,1,0:T(8,128)(2,1)S(1)}, bf16[4,64,128]{2,1,0:T(8,128)(2,1)S(1)}, u32[]{:S(2)}, u32[]{:S(2)}) collective-permute-start(bf16[4,64,128]{2,1,0:T(8,128)(2,1)S(1)} %get-tuple-element.37), channel_id=1, source_target_pairs={{0,80},{16,64},{32,112},{48,96},{64,16},{80,0},{96,48},{112,32},{1... | collective-permute-start | bytes 196616 | tf_op jit(solution)/shard_map/ppermute | solution.py:231
  60.9 8.1 %collective-permute-start.2 = (bf16[4,64,128]{2,1,0:T(8,128)(2,1)S(1)}, bf16[4,64,128]{2,1,0:T(8,128)(2,1)S(1)}, u32[]{:S(2)}, u32[]{:S(2)}) collective-permute-start(bf16[4,64,128]{2,1,0:T(8,128)(2,1)S(1)} %get-tuple-element.38), channel_id=1, source_target_pairs={{0,16},{16,0},{32,48},{48,32},{64,80},{80,64},{96,112},{112,96},{1... | collective-permute-start | bytes 196616 | tf_op jit(solution)/shard_map/ppermute | solution.py:231
  69.0 8.8 %collective-permute-start.3 = (bf16[2,64,128]{2,1,0:T(8,128)(2,1)S(1)}, bf16[2,64,128]{2,1,0:T(8,128)(2,1)S(1)}, u32[]{:S(2)}, u32[]{:S(2)}) collective-permute-start(bf16[2,64,128]{2,1,0:T(8,128)(2,1)S(1)} %slice.23), channel_id=1, source_target_pairs={{0,32},{16,48},{32,0},{48,16},{64,96},{80,112},{96,64},{112,80},{1... | collective-permute-start | bytes 98312 | tf_op jit(solution)/shard_map/ppermute | solution.py:231
